TPU v7x, 256 devices: a whole 4x4x8 slice. The times are simulated.
256 devices in a mesh: dp: 8 (over y, z_lo), tensor: 32 (over z_hi, x, core).
Axes of the slice: x: 4, y: 4, z: 8 (z_hi: 4, z_lo: 2; z = z_hi * 2 + z_lo), core: 2. Of those that a mesh axis runs over, the one named last changes fastest.
Arguments:
- query_latent: bfloat16 [2, 512, 1536], P(None, ('dp', 'tensor')), may hold values from -6 to 6
- fresh_latent: bfloat16 [2, 512, 576], P(None, ('dp', 'tensor')), may hold values from -4 to 4
- stream: bfloat16 [2, 512, 7168], P(None, ('dp', 'tensor')), may hold values from -4 to 4
- lengths: int32 [512], P(('dp', 'tensor')), may hold values from 128 to 512, as said below
- latent_cache: bfloat16 [512, 512, 576], P(('dp', 'tensor')), may hold values from -300 to 300
- w_qb: bfloat16 [1536, 24576], P('dp', 'tensor'), may hold values from -0.15625 to 0.15625
- w_uk: bfloat16 [128, 128, 512], P('tensor'), may hold values from -0.5 to 0.5
- w_uv: bfloat16 [128, 512, 128], P('tensor'), may hold values from -0.25 to 0.25
- w_o: bfloat16 [16384, 7168], P('tensor'), may hold values from -0.1875 to 0.1875
- norm_gain: bfloat16 [7168], replicated, may hold values from 0.25 to 1.75
- w_gate: bfloat16 [7168, 9216], P('dp', 'tensor'), may hold values from -0.0625 to 0.0625
- w_up: bfloat16 [7168, 9216], P('dp', 'tensor'), may hold values from -0.0625 to 0.0625
- w_down: bfloat16 [9216, 7168], P('tensor', 'dp'), may hold values from -0.0625 to 0.0625
Outputs:
- layer_out: bfloat16 [2, 512, 7168], P(None, ('dp', 'tensor'))
Inputs may be any that keep to these rules, and one draw needn't show every extreme that they name: Row n attends to its first lengths[n] cache slots; some row fills all 512 slots and some row exactly 128.
All inputs are finite; a program needn't handle non-finite values.
Results may differ from a plain program's by a relative error of at most 0.035.
Values may be sent and summed in bfloat16 or wider, within the bound.
No kernel may reach another device: no remote copies, remote signals or barrier semaphores. Data moves between devices by JAX's collectives and lax.ppermute only.
A program may use at most 128 MiB of HBM per device.

v0:
```python
import math

import jax
import jax.numpy as jnp
from jax import lax
from jax.experimental import pallas as pl
from jax.experimental.pallas import tpu as pltpu
from jax.sharding import Mesh, PartitionSpec as P

NOPE = 128
ROPE = 64
LATENT = 512
VHEAD = 128
STEPS = 2

SIZES = {"y": 4, "l": 2, "z": 4, "x": 4, "c": 2}
DP = ("y", "l")
TENSOR = ("z", "x", "c")
HEADS = ("c", "x", "z")


def shift(value, axis, by):
    size = SIZES[axis]
    return lax.ppermute(value, axis, [(i, (i + by) % size) for i in range(size)])


def nearest_first(size):
    return sorted(range(1, size), key=lambda k: min(k, size - k))


def gather_back(value, axis):
    parts = {0: value}
    for k in nearest_first(SIZES[axis]):
        parts[k] = shift(value, axis, k)
    return jnp.concatenate([parts[k] for k in range(SIZES[axis])], axis=0)


def scatter_back(parts, axis):
    total = parts[0].astype(jnp.float32)
    for by in nearest_first(SIZES[axis]):
        part = parts[SIZES[axis] - by]
        total = total + shift(part, axis, by).astype(jnp.float32)
    return total


def scatter_rows(terms):
    for axis in ("x", "z"):
        rows = terms.shape[0] // SIZES[axis]
        parts = [terms[k * rows : (k + 1) * rows] for k in range(SIZES[axis])]
        terms = scatter_back(parts, axis)
        if axis == "x":
            terms = terms.astype(jnp.bfloat16)
    return terms


def rms_scale(mixed, norm_gain):
    wide = mixed.astype(jnp.float32)
    factor = lax.rsqrt(jnp.mean(wide * wide, axis=-1, keepdims=True) + 1e-06)
    return (wide * factor * norm_gain.astype(jnp.float32)).astype(jnp.bfloat16)


def attend_rows(query, keys, lengths, turn):
    steps, rows, places, wide = query.shape
    heads = wide // (LATENT + ROPE)
    slots = keys.shape[2] - 128
    scale = (NOPE + ROPE) ** (-0.5)
    per_step = heads * places

    def body(lengths_ref, query_ref, keys_ref, turn_ref, out_ref):
        row = pl.program_id(0)
        content, rotary = [], []
        lane = lax.broadcasted_iota(jnp.int32, (places, 2 * ROPE), 1)
        first_half = lane % ROPE < ROPE // 2
        for step in range(steps):
            for head in range(heads):
                content.append(query_ref[step, 0, :, head * LATENT : (head + 1) * LATENT])
            for pair in range(heads // 2):
                at = heads * LATENT + pair * 2 * ROPE
                value = query_ref[step, 0, :, at : at + 2 * ROPE].astype(jnp.float32)
                other = jnp.where(
                    first_half,
                    pltpu.roll(value, 2 * ROPE - ROPE // 2, 1),
                    pltpu.roll(value, ROPE // 2, 1),
                )
                cosine = turn_ref[0, step, pl.ds(row, 1)]
                sine_part = turn_ref[1, step, pl.ds(row, 1)]
                value = value * cosine + other * sine_part
                rotary.append(jnp.where(lane < ROPE, value, 0.0).astype(jnp.bfloat16))
                rotary.append(jnp.where(lane < ROPE, 0.0, value).astype(jnp.bfloat16))
        content = jnp.concatenate(content, axis=0)
        rotary = jnp.concatenate(rotary, axis=0)
        latents = keys_ref[0, :LATENT]
        turned = keys_ref[0, LATENT:]
        scores = jnp.dot(content, latents, preferred_element_type=jnp.float32)
        scores += jnp.dot(
            rotary, jnp.concatenate([turned, turned], axis=0), preferred_element_type=jnp.float32
        )
        slot = lax.broadcasted_iota(jnp.int32, scores.shape, 1)
        step = lax.broadcasted_iota(jnp.int32, scores.shape, 0) // per_step
        fresh = slot - slots
        seen = (slot < lengths_ref[row]) | ((fresh >= 0) & (fresh <= step))
        scores = jnp.where(seen, scores * scale, -jnp.inf)
        weights = jnp.exp(scores - jnp.max(scores, axis=1, keepdims=True))
        probs = weights / jnp.sum(weights, axis=1, keepdims=True)
        out = lax.dot_general(
            probs.astype(jnp.bfloat16),
            latents,
            (((1,), (1,)), ((), ())),
            preferred_element_type=jnp.float32,
        ).astype(jnp.bfloat16)
        for step in range(steps):
            for head in range(heads):
                at = step * per_step + head * places
                out_ref[step, 0, :, head * LATENT : (head + 1) * LATENT] = out[at : at + places]

    return pl.pallas_call(
        body,
        grid_spec=pltpu.PrefetchScalarGridSpec(
            num_scalar_prefetch=1,
            grid=(rows,),
            in_specs=[
                pl.BlockSpec((steps, 1, places, wide), lambda r, _: (0, r, 0, 0)),
                pl.BlockSpec((1,) + keys.shape[1:], lambda r, _: (r, 0, 0)),
                pl.BlockSpec(turn.shape, lambda r, _: (0, 0, 0, 0)),
            ],
            out_specs=pl.BlockSpec((steps, 1, places, heads * LATENT), lambda r, _: (0, r, 0, 0)),
        ),
        out_shape=jax.ShapeDtypeStruct((steps, rows, places, heads * LATENT), jnp.bfloat16),
        cost_estimate=pl.CostEstimate(
            flops=4 * rows * steps * per_step * LATENT * slots,
            bytes_accessed=4 * query.size + 2 * keys.size,
            transcendentals=rows * steps * per_step * slots,
        ),
        compiler_params=pltpu.CompilerParams(vmem_limit_bytes=32 * 1024 * 1024),
    )(lengths, query, keys, turn)


def shards(
    query_latent,
    fresh_latent,
    stream,
    lengths,
    latent_cache,
    w_qb,
    w_uk,
    w_uv,
    w_o,
    norm_gain,
    w_gate,
    w_up,
    w_down,
):
    bf16 = jnp.bfloat16
    heads_here = w_uk.shape[0]
    rows_dev = lengths.shape[0]
    local = STEPS * rows_dev
    width = stream.shape[-1]
    chunk, units = w_gate.shape
    part = w_qb.shape[0]
    ny, nl, nz, nx, nc = (SIZES[a] for a in ("y", "l", "z", "x", "c"))
    here = {axis: lax.axis_index(axis) for axis in SIZES}
    l_index = here["l"]
    turned = jnp.stack(
        [
            ((here["c"] - c) % nc * nx + (here["x"] - x) % nx) * nz + (here["z"] - z) % nz
            for c in range(nc)
            for x in range(nx)
            for z in range(nz)
        ]
    )

    def by_pair(kept, sent):
        sent = shift(sent, "l", 1)
        return jnp.where(l_index == 0, kept, sent), jnp.where(l_index == 0, sent, kept)

    query_weights = lax.all_gather(w_qb, "y", axis=0, tiled=True)
    split = query_latent.reshape(local, ny, nl, part)
    kept = lax.dynamic_index_in_dim(split, l_index, axis=2, keepdims=False)
    sent = lax.dynamic_index_in_dim(split, 1 - l_index, axis=2, keepdims=False)
    pair = by_pair(kept.reshape(local, ny * part), sent.reshape(local, ny * part))
    everyone = gather_back(jnp.concatenate(pair, axis=0), "z")

    packed = jnp.concatenate([w_gate.T, w_up.T, w_down], axis=0)
    everyone, packed = lax.optimization_barrier((everyone, packed))
    weights = lax.all_gather(packed, "y", axis=1, tiled=True)
    everyone = gather_back(gather_back(everyone, "x"), "c")

    projected = jnp.dot(everyone, query_weights, preferred_element_type=jnp.float32)
    projected = projected.reshape(nc * nx * nz, nl, local, projected.shape[-1])
    kept = jnp.where(l_index == 0, projected[:, 0], projected[:, 1])
    sent = jnp.where(l_index == 0, projected[:, 1], projected[:, 0]).astype(bf16)
    projected = kept + shift(sent, "l", 1).astype(jnp.float32)
    projected = projected.astype(bf16).reshape(-1, heads_here, NOPE + ROPE)
    absorbed = jnp.einsum(
        "nhd,hdc->nhc", projected[..., :NOPE], w_uk, preferred_element_type=jnp.float32
    ).astype(bf16)
    query = jnp.concatenate(
        [
            absorbed.reshape(-1, heads_here * LATENT),
            projected[..., NOPE:].reshape(-1, heads_here * ROPE),
        ],
        axis=1,
    )
    query = query.reshape(nc * nx * nz, local, heads_here * (LATENT + ROPE))
    query = lax.all_to_all(jnp.take(query, turned, axis=0, mode="clip"), HEADS, 0, 0, tiled=True)

    fresh = jnp.transpose(fresh_latent, (1, 2, 0))
    keys = jnp.concatenate(
        [
            jnp.swapaxes(latent_cache, 1, 2),
            jnp.pad(fresh, ((0, 0), (0, 0), (0, 128 - STEPS))),
        ],
        axis=2,
    )
    ladder = jnp.arange(ROPE // 2).astype(jnp.float32)
    frequency = jnp.exp(ladder * (-2.0 * math.log(10000.0) / ROPE))
    position = (lengths[None, :] + jnp.arange(STEPS)[:, None]).astype(jnp.float32)
    angle = position[:, :, None] * frequency
    cosine, sine_part = jnp.cos(angle), jnp.sin(angle)
    turn = jnp.stack(
        [
            jnp.concatenate([cosine, cosine, cosine, cosine], axis=-1),
            jnp.concatenate([-sine_part, sine_part, -sine_part, sine_part], axis=-1),
        ]
    )
    query, keys, turn = lax.optimization_barrier((query, keys, turn))
    query = query.reshape(-1, STEPS, rows_dev, query.shape[-1]).transpose(1, 2, 0, 3)
    attended = attend_rows(query, keys, lengths, turn)
    attended = attended.transpose(2, 0, 1, 3).reshape(-1, local, heads_here * LATENT)

    returned = lax.all_to_all(attended, HEADS, 0, 0, tiled=True)
    returned = returned.reshape(-1, heads_here, LATENT)
    head_values = jnp.einsum(
        "nhc,hcv->nhv", returned, w_uv, preferred_element_type=jnp.float32
    ).astype(bf16)
    head_values = head_values.reshape(nc * nx * nz, local * heads_here * VHEAD)
    head_values = jnp.take(head_values, turned, axis=0, mode="clip").reshape(-1, heads_here * VHEAD)
    terms = jnp.dot(head_values, w_o, preferred_element_type=jnp.float32).astype(bf16)
    terms, weights = lax.optimization_barrier((terms, weights))
    half = terms.shape[0] // 2
    terms = terms[:half].astype(jnp.float32) + shift(terms[half:], "c", 1).astype(jnp.float32)
    attention_out = scatter_rows(terms.astype(bf16))
    mixed = (stream.reshape(local, width).astype(jnp.float32) + attention_out).astype(bf16)
    normed = rms_scale(mixed, norm_gain)

    split = normed.reshape(local, ny, nl, chunk)
    kept = lax.dynamic_index_in_dim(split, l_index, axis=2, keepdims=False)
    sent = lax.dynamic_index_in_dim(split, 1 - l_index, axis=2, keepdims=False)
    pair = by_pair(kept.reshape(local, ny * chunk), sent.reshape(local, ny * chunk))
    first = lax.optimization_barrier(gather_back(jnp.concatenate(pair, axis=0), "z"))
    first = lax.optimization_barrier(gather_back(first, "x"))
    second = shift(first, "c", 1)

    def gate_up(rows):
        return lax.dot_general(
            rows,
            weights[: 2 * units],
            (((1,), (1,)), ((), ())),
            preferred_element_type=jnp.float32,
        )

    def down(both, away):
        both = both + away.astype(jnp.float32)
        hidden = (jax.nn.silu(both[:, :units]) * both[:, units:]).astype(bf16)
        return jnp.dot(hidden, weights[2 * units :], preferred_element_type=jnp.float32)

    first, second = gate_up(first), gate_up(second)
    first_away = shift(first.astype(bf16), "l", 1)
    second_away = shift(second.astype(bf16), "l", 1)
    first_away, second_away = lax.optimization_barrier((first_away, second_away))
    away = shift(down(second, second_away).astype(bf16), "c", 1)
    terms = down(first, first_away) + away.astype(jnp.float32)
    value = scatter_rows(terms.astype(bf16))
    sent = jnp.where(l_index == 0, value[local:], value[:local]).astype(bf16)
    value = jnp.where(l_index == 0, value[:local], value[local:])
    sent = shift(sent, "l", 1).astype(jnp.float32)
    value = jnp.stack(
        [
            jnp.where(l_index == 0, value, sent).reshape(local, ny, chunk),
            jnp.where(l_index == 0, sent, value).reshape(local, ny, chunk),
        ],
        axis=2,
    ).reshape(local, width)
    out = (mixed.astype(jnp.float32) + value).astype(bf16)
    return out.reshape(STEPS, rows_dev, width)


def solution(mesh):
    parts = Mesh(mesh.devices.reshape(tuple(SIZES.values())), tuple(SIZES))
    rows = P(None, DP + TENSOR, None)
    placed = (
        rows,
        rows,
        rows,
        P(DP + TENSOR),
        P(DP + TENSOR, None, None),
        P(DP, TENSOR),
        P(TENSOR, None, None),
        P(TENSOR, None, None),
        P(TENSOR, None),
        P(),
        P(DP, TENSOR),
        P(DP, TENSOR),
        P(TENSOR, DP),
    )
    return jax.shard_map(
        shards, mesh=parts, in_specs=placed, out_specs=rows, check_vma=False
    )
```

profile of v0, /device:TPU:1, one launch (start us, length us, event | category | flops | bytes accessed | tf_op | source)
XLA Modules:
  0.0 222.2 jit_solution(13392247906309629080)
XLA Ops:
  11.9 3.1 %collective-permute-start.1 = (bf16[8,768]{1,0:T(8,128)(2,1)S(1)}, bf16[8,768]{1,0:T(8,128)(2,1)S(1)}, u32[]{:S(2)}, u32[]{:S(2)}) collective-permute-start(bf16[8,768]{1,0:T(8,128)(2,1)S(1)} %pad_maximum_fusion.6), channel_id=1, source_target_pairs={{0,8},{8,16},{16,24},{24,0},{1,9},{9,17},{17,25},{25,1},{2,10},{10... | collective-permute-start | bytes 36872 | tf_op jit(solution)/shard_map/ppermute | solution.py:24
  14.9 4.9 %collective-permute-start.2 = (bf16[8,768]{1,0:T(8,128)(2,1)S(1)}, bf16[8,768]{1,0:T(8,128)(2,1)S(1)}, u32[]{:S(2)}, u32[]{:S(2)}) collective-permute-start(bf16[8,768]{1,0:T(8,128)(2,1)S(1)} %pad_maximum_fusion.6), channel_id=1, source_target_pairs={{0,16},{8,24},{16,0},{24,8},{1,17},{9,25},{17,1},{25,9},{2,18},{10... | collective-permute-start | bytes 36872 | tf_op jit(solution)/shard_map/ppermute | solution.py:24
  32.0 4.1 %collective-permute-start.7 = (bf16[128,768]{1,0:T(8,128)(2,1)S(1)}, bf16[128,768]{1,0:T(8,128)(2,1)S(1)}, u32[]{:S(2)}, u32[]{:S(2)}) collective-permute-start(bf16[128,768]{1,0:T(8,128)(2,1)S(1)} %pad_maximum_fusion.3), channel_id=1, source_target_pairs={{0,1},{1,0},{2,3},{3,2},{4,5},{5,4},{6,7},{7,6},{8,9},{9,8},{10,11... | collective-permute-start | bytes 589832 | tf_op jit(solution)/shard_map/ppermute | solution.py:24
  42.6 3.1 %collective-permute-done.8 = bf16[32,4,768]{2,1,0:T(4,128)(2,1)S(1)} collective-permute-done((bf16[32,4,768]{2,1,0:T(4,128)(2,1)S(1)}, bf16[32,4,768]{2,1,0:T(4,128)(2,1)S(1)}, u32[]{:S(2)}, u32[]{:S(2)}) %collective-permute-start.8) | collective-permute-done | bytes 196640 | tf_op jit(solution)/shard_map/ppermute | solution.py:24
  49.6 12.4 %all-to-all-start = ((bf16[32,4,2304]{2,1,0:T(4,128)(2,1)}), bf16[32,4,2304]{2,1,0:T(4,128)(2,1)S(1)}, u32[]{:S(2)}, u32[]{:S(2)}) async-start(bf16[32,4,2304]{2,1,0:T(4,128)(2,1)} %gather_fusion), calls=%async_computation | async-start | bytes 1179648 | tf_op jit(solution)/shard_map/all_to_all | solution.py:205
  63.9 17.0 %all-to-all-done = bf16[32,4,2304]{2,1,0:T(4,128)(2,1)S(1)} async-done(((bf16[32,4,2304]{2,1,0:T(4,128)(2,1)}), bf16[32,4,2304]{2,1,0:T(4,128)(2,1)S(1)}, u32[]{:S(2)}, u32[]{:S(2)}) %all-to-all-start) | async-done | bytes 589856 | tf_op jit(solution)/shard_map/all_to_all | solution.py:205
  80.9 2.7 %shard_map.127 = bf16[2,2,32,2048]{3,2,1,0:T(8,128)(2,1)S(1)} custom-call(s32[2]{0:T(128)S(1)} %copy-done.1, bf16[2,2,32,2304]{3,2,1,0:T(8,128)(2,1)S(1)} %bitcast.84, bf16[2,576,640]{2,1,0:T(8,128)(2,1)S(1)} %fusion.10.keys_ref, f32[2,2,2,128]{3,2,1,0:T(2,128)S(1)} %pad_maximum_fusion.7.turn_ref), custom_call_target="tpu_custom_call" | custom-call | flops 536870912 | bytes 2654208 | tf_op jit(solution)/shard_map/pallas_call | solution.py:116
  84.0 22.2 %all_to_all.10 = bf16[32,4,2048]{2,1,0:T(4,128)(2,1)S(1)} all-to-all(bf16[32,4,2048]{2,1,0:T(4,128)(2,1)S(1)} %copy.29), channel_id=1, replica_groups=mesh['y'=4,'l'=2,'z'=4,'x'=4,'c'=2] {'c','x','z'}, dimensions={0} | all-to-all | bytes 1048576 | tf_op jit(solution)/shard_map/all_to_all | solution.py:231
  107.9 4.2 %convolution_convert_fusion = bf16[128,7168]{1,0:T(8,128)(2,1)S(1)} fusion(bf16[128,512]{1,0:T(8,128)(2,1)S(1)} %reshape.107, bf16[512,7168]{1,0:T(8,128)(2,1)} %param.21), kind=kOutput, calls=%fused_computation.2 | convolution fusion | flops 940441600 | bytes 9306112 | tf_op jit(solution)/shard_map/dot_general | solution.py:238
  119.6 4.9 %collective-permute-done.10 = bf16[16,7168]{1,0:T(8,128)(2,1)S(1)} collective-permute-done((bf16[16,7168]{1,0:T(8,128)(2,1)S(1)}, bf16[16,7168]{1,0:T(8,128)(2,1)S(1)}, u32[]{:S(2)}, u32[]{:S(2)}) %collective-permute-start.10) | collective-permute-done | bytes 229408 | tf_op jit(solution)/shard_map/ppermute | solution.py:24
  124.5 4.2 %collective-permute-done.12 = bf16[16,7168]{1,0:T(8,128)(2,1)S(1)} collective-permute-done((bf16[16,7168]{1,0:T(8,128)(2,1)S(1)}, bf16[16,7168]{1,0:T(8,128)(2,1)S(1)}, u32[]{:S(2)}, u32[]{:S(2)}) %collective-permute-start.12) | collective-permute-done | bytes 229408 | tf_op jit(solution)/shard_map/ppermute | solution.py:24
  132.6 3.7 %collective-permute-start.15 = (bf16[4,7168]{1,0:T(4,128)(2,1)S(1)}, bf16[4,7168]{1,0:T(4,128)(2,1)S(1)}, u32[]{:S(2)}, u32[]{:S(2)}) collective-permute-start(bf16[4,7168]{1,0:T(4,128)(2,1)S(1)} %get-tuple-element.39), channel_id=1, source_target_pairs={{0,16},{8,24},{16,0},{24,8},{1,17},{9,25},{17,1},{25,9},{2,18},{10... | collective-permute-start | bytes 172040 | tf_op jit(solution)/shard_map/ppermute | solution.py:24
  136.4 3.2 %collective-permute-done.15 = bf16[4,7168]{1,0:T(4,128)(2,1)S(1)} collective-permute-done((bf16[4,7168]{1,0:T(4,128)(2,1)S(1)}, bf16[4,7168]{1,0:T(4,128)(2,1)S(1)}, u32[]{:S(2)}, u32[]{:S(2)}) %collective-permute-start.15) | collective-permute-done | bytes 57376 | tf_op jit(solution)/shard_map/ppermute | solution.py:24
  143.7 3.7 %collective-permute-start.18 = (bf16[8,3584]{1,0:T(8,128)(2,1)S(1)}, bf16[8,3584]{1,0:T(8,128)(2,1)S(1)}, u32[]{:S(2)}, u32[]{:S(2)}) collective-permute-start(bf16[8,3584]{1,0:T(8,128)(2,1)S(1)} %pad_maximum_fusion.5), channel_id=1, source_target_pairs={{0,16},{8,24},{16,0},{24,8},{1,17},{9,25},{17,1},{25,9},{2,18},{10... | collective-permute-start | bytes 172040 | tf_op jit(solution)/shard_map/ppermute | solution.py:24
  147.4 3.5 %collective-permute-start.19 = (bf16[8,3584]{1,0:T(8,128)(2,1)S(1)}, bf16[8,3584]{1,0:T(8,128)(2,1)S(1)}, u32[]{:S(2)}, u32[]{:S(2)}) collective-permute-start(bf16[8,3584]{1,0:T(8,128)(2,1)S(1)} %pad_maximum_fusion.5), channel_id=1, source_target_pairs={{0,24},{8,0},{16,8},{24,16},{1,25},{9,1},{17,9},{25,17},{2,26},{10... | collective-permute-start | bytes 172040 | tf_op jit(solution)/shard_map/ppermute | solution.py:24
  158.8 2.8 %collective-permute-done.21 = bf16[32,3584]{1,0:T(8,128)(2,1)S(1)} collective-permute-done((bf16[32,3584]{1,0:T(8,128)(2,1)S(1)}, bf16[32,3584]{1,0:T(8,128)(2,1)S(1)}, u32[]{:S(2)}, u32[]{:S(2)}) %collective-permute-start.21) | collective-permute-done | bytes 229408 | tf_op jit(solution)/shard_map/ppermute | solution.py:24
  161.9 7.5 %collective-permute-start.24 = (bf16[128,3584]{1,0:T(8,128)(2,1)S(1)}, bf16[128,3584]{1,0:T(8,128)(2,1)S(1)}, u32[]{:S(2)}, u32[]{:S(2)}) collective-permute-start(bf16[128,3584]{1,0:T(8,128)(2,1)S(1)} %pad_maximum_fusion.1), channel_id=1, source_target_pairs={{0,1},{1,0},{2,3},{3,2},{4,5},{5,4},{6,7},{7,6},{8,9},{9,8},{10,11... | collective-permute-start | bytes 2752520 | tf_op jit(solution)/shard_map/ppermute | solution.py:24
  169.4 3.4 %fusion.34 = (bf16[128,576]{0,1:T(8,128)(2,1)S(1)}, f32[128,576]{0,1:T(8,128)S(1)}) fusion(bf16[128,3584]{1,0:T(8,128)(2,1)S(1)} %pad_maximum_fusion.1, bf16[864,3584]{1,0:T(8,128)(2,1)} %all-gather.5.cloned.1.call-done), kind=kOutput, calls=%fused_computation.87 | convolution fusion | flops 528556032 | bytes 5488640 | tf_op jit(solution)/shard_map/dot_general | solution.py:255
  175.6 2.7 %collective-permute-done.23 = bf16[128,576]{0,1:T(8,128)(2,1)S(1)} collective-permute-done((bf16[128,576]{0,1:T(8,128)(2,1)S(1)}, bf16[128,576]{0,1:T(8,128)(2,1)S(1)}, u32[]{:S(2)}, u32[]{:S(2)}) %collective-permute-start.23) | collective-permute-done | bytes 147488 | tf_op jit(solution)/shard_map/ppermute | solution.py:24
  178.3 3.2 %collective-permute-done.25 = bf16[128,576]{0,1:T(8,128)(2,1)S(1)} collective-permute-done((bf16[128,576]{0,1:T(8,128)(2,1)S(1)}, bf16[128,576]{0,1:T(8,128)(2,1)S(1)}, u32[]{:S(2)}, u32[]{:S(2)}) %collective-permute-start.25) | collective-permute-done | bytes 147488 | tf_op jit(solution)/shard_map/ppermute | solution.py:24
  189.6 4.5 %collective-permute-done.27 = bf16[32,3584]{1,0:T(8,128)(2,1)S(1)} collective-permute-done((bf16[32,3584]{1,0:T(8,128)(2,1)S(1)}, bf16[32,3584]{1,0:T(8,128)(2,1)S(1)}, u32[]{:S(2)}, u32[]{:S(2)}) %collective-permute-start.27) | collective-permute-done | bytes 229408 | tf_op jit(solution)/shard_map/ppermute | solution.py:24
  194.1 5.8 %collective-permute-done.29 = bf16[32,3584]{1,0:T(8,128)(2,1)S(1)} collective-permute-done((bf16[32,3584]{1,0:T(8,128)(2,1)S(1)}, bf16[32,3584]{1,0:T(8,128)(2,1)S(1)}, u32[]{:S(2)}, u32[]{:S(2)}) %collective-permute-start.29) | collective-permute-done | bytes 229408 | tf_op jit(solution)/shard_map/ppermute | solution.py:24
  200.0 3.1 %collective-permute-start.30 = (bf16[8,3584]{1,0:T(8,128)(2,1)S(1)}, bf16[8,3584]{1,0:T(8,128)(2,1)S(1)}, u32[]{:S(2)}, u32[]{:S(2)}) collective-permute-start(bf16[8,3584]{1,0:T(8,128)(2,1)S(1)} %get-tuple-element.35), channel_id=1, source_target_pairs={{0,8},{8,16},{16,24},{24,0},{1,9},{9,17},{17,25},{25,1},{2,10},{10... | collective-permute-start | bytes 172040 | tf_op jit(solution)/shard_map/ppermute | solution.py:24
  207.6 3.7 %collective-permute-done.32 = bf16[8,3584]{1,0:T(8,128)(2,1)S(1)} collective-permute-done((bf16[8,3584]{1,0:T(8,128)(2,1)S(1)}, bf16[8,3584]{1,0:T(8,128)(2,1)S(1)}, u32[]{:S(2)}, u32[]{:S(2)}) %collective-permute-start.32) | collective-permute-done | bytes 57376 | tf_op jit(solution)/shard_map/ppermute | solution.py:24
  (152 shorter events, 74.7 us)
Async XLA Ops:
  6.5 32.5 %all-gather.3.cloned.1.call-start = ((), (), s32[]{:S(2)}) async-start(), calls=%async_computation.2 | async-start | bytes 1474560 | tf_op jit(solution)/shard_map/all_gather | solution.py:176
  7.3 104.9 %all-gather.5.cloned.1.call-start = ((), (), s32[]{:S(2)}) async-start(), calls=%async_computation.3 | async-start | bytes 7741440 | tf_op jit(solution)/shard_map/all_gather | solution.py:185
  11.9 13.0 %collective-permute-start.1 = (bf16[8,768]{1,0:T(8,128)(2,1)S(1)}, bf16[8,768]{1,0:T(8,128)(2,1)S(1)}, u32[]{:S(2)}, u32[]{:S(2)}) collective-permute-start(bf16[8,768]{1,0:T(8,128)(2,1)S(1)} %pad_maximum_fusion.6), channel_id=1, source_target_pairs={{0,8},{8,16},{16,24},{24,0},{1,9},{9,17},{17,25},{25,1},{2,10},{10... | collective-permute-start | bytes 36872 | tf_op jit(solution)/shard_map/ppermute | solution.py:24
  14.9 10.0 %collective-permute-start.2 = (bf16[8,768]{1,0:T(8,128)(2,1)S(1)}, bf16[8,768]{1,0:T(8,128)(2,1)S(1)}, u32[]{:S(2)}, u32[]{:S(2)}) collective-permute-start(bf16[8,768]{1,0:T(8,128)(2,1)S(1)} %pad_maximum_fusion.6), channel_id=1, source_target_pairs={{0,16},{8,24},{16,0},{24,8},{1,17},{9,25},{17,1},{25,9},{2,18},{10... | collective-permute-start | bytes 36872 | tf_op jit(solution)/shard_map/ppermute | solution.py:24
  49.6 31.3 %all-to-all-start = ((bf16[32,4,2304]{2,1,0:T(4,128)(2,1)}), bf16[32,4,2304]{2,1,0:T(4,128)(2,1)S(1)}, u32[]{:S(2)}, u32[]{:S(2)}) async-start(bf16[32,4,2304]{2,1,0:T(4,128)(2,1)} %gather_fusion), calls=%async_computation | async-start | bytes 1179648 | tf_op jit(solution)/shard_map/all_to_all | solution.py:205
  116.1 8.5 %collective-permute-start.10 = (bf16[16,7168]{1,0:T(8,128)(2,1)S(1)}, bf16[16,7168]{1,0:T(8,128)(2,1)S(1)}, u32[]{:S(2)}, u32[]{:S(2)}) collective-permute-start(bf16[16,7168]{1,0:T(8,128)(2,1)S(1)} %get-tuple-element.32), channel_id=1, source_target_pairs={{0,2},{2,4},{4,6},{6,0},{1,3},{3,5},{5,7},{7,1},{8,10},{10,12},{12... | collective-permute-start | bytes 688136 | tf_op jit(solution)/shard_map/ppermute | solution.py:24
  116.9 7.6 %collective-permute-start.11 = (bf16[16,7168]{1,0:T(8,128)(2,1)S(1)}, bf16[16,7168]{1,0:T(8,128)(2,1)S(1)}, u32[]{:S(2)}, u32[]{:S(2)}) collective-permute-start(bf16[16,7168]{1,0:T(8,128)(2,1)S(1)} %get-tuple-element.34), channel_id=1, source_target_pairs={{0,6},{2,0},{4,2},{6,4},{1,7},{3,1},{5,3},{7,5},{8,14},{10,8},{12,... | collective-permute-start | bytes 688136 | tf_op jit(solution)/shard_map/ppermute | solution.py:24
  118.8 9.9 %collective-permute-start.12 = (bf16[16,7168]{1,0:T(8,128)(2,1)S(1)}, bf16[16,7168]{1,0:T(8,128)(2,1)S(1)}, u32[]{:S(2)}, u32[]{:S(2)}) collective-permute-start(bf16[16,7168]{1,0:T(8,128)(2,1)S(1)} %get-tuple-element.33), channel_id=1, source_target_pairs={{0,4},{2,6},{4,0},{6,2},{1,5},{3,7},{5,1},{7,3},{8,12},{10,14},{12... | collective-permute-start | bytes 688136 | tf_op jit(solution)/shard_map/ppermute | solution.py:24
  129.0 7.4 %collective-permute-start.13 = (bf16[4,7168]{1,0:T(4,128)(2,1)S(1)}, bf16[4,7168]{1,0:T(4,128)(2,1)S(1)}, u32[]{:S(2)}, u32[]{:S(2)}) collective-permute-start(bf16[4,7168]{1,0:T(4,128)(2,1)S(1)} %get-tuple-element.38), channel_id=1, source_target_pairs={{0,8},{8,16},{16,24},{24,0},{1,9},{9,17},{17,25},{25,1},{2,10},{10... | collective-permute-start | bytes 172040 | tf_op jit(solution)/shard_map/ppermute | solution.py:24
  130.5 5.9 %collective-permute-start.14 = (bf16[4,7168]{1,0:T(4,128)(2,1)S(1)}, bf16[4,7168]{1,0:T(4,128)(2,1)S(1)}, u32[]{:S(2)}, u32[]{:S(2)}) collective-permute-start(bf16[4,7168]{1,0:T(4,128)(2,1)S(1)} %get-tuple-element.40), channel_id=1, source_target_pairs={{0,24},{8,0},{16,8},{24,16},{1,25},{9,1},{17,9},{25,17},{2,26},{10... | collective-permute-start | bytes 172040 | tf_op jit(solution)/shard_map/ppermute | solution.py:24
  132.6 6.9 %collective-permute-start.15 = (bf16[4,7168]{1,0:T(4,128)(2,1)S(1)}, bf16[4,7168]{1,0:T(4,128)(2,1)S(1)}, u32[]{:S(2)}, u32[]{:S(2)}) collective-permute-start(bf16[4,7168]{1,0:T(4,128)(2,1)S(1)} %get-tuple-element.39), channel_id=1, source_target_pairs={{0,16},{8,24},{16,0},{24,8},{1,17},{9,25},{17,1},{25,9},{2,18},{10... | collective-permute-start | bytes 172040 | tf_op jit(solution)/shard_map/ppermute | solution.py:24
  143.2 7.7 %collective-permute-start.17 = (bf16[8,3584]{1,0:T(8,128)(2,1)S(1)}, bf16[8,3584]{1,0:T(8,128)(2,1)S(1)}, u32[]{:S(2)}, u32[]{:S(2)}) collective-permute-start(bf16[8,3584]{1,0:T(8,128)(2,1)S(1)} %pad_maximum_fusion.5), channel_id=1, source_target_pairs={{0,8},{8,16},{16,24},{24,0},{1,9},{9,17},{17,25},{25,1},{2,10},{10... | collective-permute-start | bytes 172040 | tf_op jit(solution)/shard_map/ppermute | solution.py:24
  143.7 7.2 %collective-permute-start.18 = (bf16[8,3584]{1,0:T(8,128)(2,1)S(1)}, bf16[8,3584]{1,0:T(8,128)(2,1)S(1)}, u32[]{:S(2)}, u32[]{:S(2)}) collective-permute-start(bf16[8,3584]{1,0:T(8,128)(2,1)S(1)} %pad_maximum_fusion.5), channel_id=1, source_target_pairs={{0,16},{8,24},{16,0},{24,8},{1,17},{9,25},{17,1},{25,9},{2,18},{10... | collective-permute-start | bytes 172040 | tf_op jit(solution)/shard_map/ppermute | solution.py:24
  152.6 6.2 %collective-permute-start.20 = (bf16[32,3584]{1,0:T(8,128)(2,1)S(1)}, bf16[32,3584]{1,0:T(8,128)(2,1)S(1)}, u32[]{:S(2)}, u32[]{:S(2)}) collective-permute-start(bf16[32,3584]{1,0:T(8,128)(2,1)S(1)} %concatenate.56), channel_id=1, source_target_pairs={{0,2},{2,4},{4,6},{6,0},{1,3},{3,5},{5,7},{7,1},{8,10},{10,12},{12... | collective-permute-start | bytes 688136 | tf_op jit(solution)/shard_map/ppermute | solution.py:24
  154.1 7.4 %collective-permute-start.21 = (bf16[32,3584]{1,0:T(8,128)(2,1)S(1)}, bf16[32,3584]{1,0:T(8,128)(2,1)S(1)}, u32[]{:S(2)}, u32[]{:S(2)}) collective-permute-start(bf16[32,3584]{1,0:T(8,128)(2,1)S(1)} %concatenate.56), channel_id=1, source_target_pairs={{0,4},{2,6},{4,0},{6,2},{1,5},{3,7},{5,1},{7,3},{8,12},{10,14},{12... | collective-permute-start | bytes 688136 | tf_op jit(solution)/shard_map/ppermute | solution.py:24
  155.7 6.1 %collective-permute-start.22 = (bf16[32,3584]{1,0:T(8,128)(2,1)S(1)}, bf16[32,3584]{1,0:T(8,128)(2,1)S(1)}, u32[]{:S(2)}, u32[]{:S(2)}) collective-permute-start(bf16[32,3584]{1,0:T(8,128)(2,1)S(1)} %concatenate.56), channel_id=1, source_target_pairs={{0,6},{2,0},{4,2},{6,4},{1,7},{3,1},{5,3},{7,5},{8,14},{10,8},{12,... | collective-permute-start | bytes 688136 | tf_op jit(solution)/shard_map/ppermute | solution.py:24
  161.9 11.0 %collective-permute-start.24 = (bf16[128,3584]{1,0:T(8,128)(2,1)S(1)}, bf16[128,3584]{1,0:T(8,128)(2,1)S(1)}, u32[]{:S(2)}, u32[]{:S(2)}) collective-permute-start(bf16[128,3584]{1,0:T(8,128)(2,1)S(1)} %pad_maximum_fusion.1), channel_id=1, source_target_pairs={{0,1},{1,0},{2,3},{3,2},{4,5},{5,4},{6,7},{7,6},{8,9},{9,8},{10,11... | collective-permute-start | bytes 2752520 | tf_op jit(solution)/shard_map/ppermute | solution.py:24
  172.8 5.6 %collective-permute-start.23 = (bf16[128,576]{0,1:T(8,128)(2,1)S(1)}, bf16[128,576]{0,1:T(8,128)(2,1)S(1)}, u32[]{:S(2)}, u32[]{:S(2)}) collective-permute-start(bf16[128,576]{0,1:T(8,128)(2,1)S(1)} %get-tuple-element.50), channel_id=1, source_target_pairs={{0,32},{32,0},{1,33},{33,1},{2,34},{34,2},{3,35},{35,3},{4,36},{36... | collective-permute-start | bytes 442376 | tf_op jit(solution)/shard_map/ppermute | solution.py:24
  174.1 7.3 %collective-permute-start.25 = (bf16[128,576]{0,1:T(8,128)(2,1)S(1)}, bf16[128,576]{0,1:T(8,128)(2,1)S(1)}, u32[]{:S(2)}, u32[]{:S(2)}) collective-permute-start(bf16[128,576]{0,1:T(8,128)(2,1)S(1)} %get-tuple-element.52), channel_id=1, source_target_pairs={{0,32},{32,0},{1,33},{33,1},{2,34},{34,2},{3,35},{35,3},{4,36},{36... | collective-permute-start | bytes 442376 | tf_op jit(solution)/shard_map/ppermute | solution.py:24
  186.0 8.1 %collective-permute-start.27 = (bf16[32,3584]{1,0:T(8,128)(2,1)S(1)}, bf16[32,3584]{1,0:T(8,128)(2,1)S(1)}, u32[]{:S(2)}, u32[]{:S(2)}) collective-permute-start(bf16[32,3584]{1,0:T(8,128)(2,1)S(1)} %get-tuple-element.29), channel_id=1, source_target_pairs={{0,2},{2,4},{4,6},{6,0},{1,3},{3,5},{5,7},{7,1},{8,10},{10,12},{12... | collective-permute-start | bytes 688136 | tf_op jit(solution)/shard_map/ppermute | solution.py:24
  186.6 7.5 %collective-permute-start.28 = (bf16[32,3584]{1,0:T(8,128)(2,1)S(1)}, bf16[32,3584]{1,0:T(8,128)(2,1)S(1)}, u32[]{:S(2)}, u32[]{:S(2)}) collective-permute-start(bf16[32,3584]{1,0:T(8,128)(2,1)S(1)} %get-tuple-element.31), channel_id=1, source_target_pairs={{0,6},{2,0},{4,2},{6,4},{1,7},{3,1},{5,3},{7,5},{8,14},{10,8},{12,... | collective-permute-start | bytes 688136 | tf_op jit(solution)/shard_map/ppermute | solution.py:24
  188.7 11.1 %collective-permute-start.29 = (bf16[32,3584]{1,0:T(8,128)(2,1)S(1)}, bf16[32,3584]{1,0:T(8,128)(2,1)S(1)}, u32[]{:S(2)}, u32[]{:S(2)}) collective-permute-start(bf16[32,3584]{1,0:T(8,128)(2,1)S(1)} %get-tuple-element.30), channel_id=1, source_target_pairs={{0,4},{2,6},{4,0},{6,2},{1,5},{3,7},{5,1},{7,3},{8,12},{10,14},{12... | collective-permute-start | bytes 688136 | tf_op jit(solution)/shard_map/ppermute | solution.py:24
  200.0 6.8 %collective-permute-start.30 = (bf16[8,3584]{1,0:T(8,128)(2,1)S(1)}, bf16[8,3584]{1,0:T(8,128)(2,1)S(1)}, u32[]{:S(2)}, u32[]{:S(2)}) collective-permute-start(bf16[8,3584]{1,0:T(8,128)(2,1)S(1)} %get-tuple-element.35), channel_id=1, source_target_pairs={{0,8},{8,16},{16,24},{24,0},{1,9},{9,17},{17,25},{25,1},{2,10},{10... | collective-permute-start | bytes 172040 | tf_op jit(solution)/shard_map/ppermute | solution.py:24
  204.4 6.9 %collective-permute-start.32 = (bf16[8,3584]{1,0:T(8,128)(2,1)S(1)}, bf16[8,3584]{1,0:T(8,128)(2,1)S(1)}, u32[]{:S(2)}, u32[]{:S(2)}) collective-permute-start(bf16[8,3584]{1,0:T(8,128)(2,1)S(1)} %get-tuple-element.36), channel_id=1, source_target_pairs={{0,16},{8,24},{16,0},{24,8},{1,17},{9,25},{17,1},{25,9},{2,18},{10... | collective-permute-start | bytes 172040 | tf_op jit(solution)/shard_map/ppermute | solution.py:24
  (21 other events, 263.0 us)
Sparse Core Ops, SparseCore 0:
  9.2 29.8 all-gather.2
  40.8 68.9 all-gather.4
where the time goes:
time: 225 us; the launch traced here: 222 us
  starting transfers between devices  80.9 us (36%)
  waiting for transfers between devices  75.5 us (34%)
  blocking collectives  22.2 us (10%)
  between operations  14 us (6%)
  matrix products  12.6 us (6%)
  local copies, waits for them, and re-layouts  8.24 us (4%)
  other arithmetic  6.04 us (3%)
  Pallas kernels  2.68 us (1%)
    ppermute x34, starting transfers between devices, shift(): lax.ppermute(value, axis, [(i, (i + by) % size) for i in range(size)])  68.5 us
    ppermute x34, waiting for transfers between devices, shift(): lax.ppermute(value, axis, [(i, (i + by) % size) for i in range(size)])  56 us
    all_to_all x1, blocking collectives, shards(): returned = lax.all_to_all(attended, HEADS, 0, 0, tiled=True)  22.2 us
    all_to_all x1, waiting for transfers between devices, shards(): lax.all_to_all(jnp.take(query, turned, axis=0, mode='clip'), HEADS, 0, 0,...  17 us
    all_to_all x1, starting transfers between devices, shards(): lax.all_to_all(jnp.take(query, turned, axis=0, mode='clip'), HEADS, 0, 0,...  12.4 us
    dot_general x2, matrix products, gate_up(): lax.dot_general(rows, weights[:2 * units], (((1,), (1,)), ((), ())), pref...  4.62 us
  transfers between devices with their start and end apart: 37, of which 24 were waited for; matrix products, arithmetic and copies ran while one was open for 10% of the time, Pallas kernels for 1%

commit v1 on v0

--- a/solution.py
+++ b/solution.py
@@ -57,6 +57,44 @@
     wide = mixed.astype(jnp.float32)
     factor = lax.rsqrt(jnp.mean(wide * wide, axis=-1, keepdims=True) + 1e-06)
     return (wide * factor * norm_gain.astype(jnp.float32)).astype(jnp.bfloat16)
+
+
+def absorb_rows(kept, away, w_uk, places):
+    heads = w_uk.shape[0]
+    blocks = places.shape[0]
+    rows = kept.shape[0] // blocks
+    wide = heads * (LATENT + ROPE)
+
+    def body(places_ref, kept_ref, away_ref, w_ref, out_ref):
+        projected = (kept_ref[...] + away_ref[...].astype(jnp.float32)).astype(jnp.bfloat16)
+        content, rotary = [], []
+        for head in range(heads):
+            at = head * (NOPE + ROPE)
+            content.append(
+                jnp.dot(
+                    projected[:, at : at + NOPE], w_ref[head], preferred_element_type=jnp.float32
+                )
+            )
+            rotary.append(projected[:, at + NOPE : at + NOPE + ROPE].astype(jnp.float32))
+        query = jnp.concatenate(content + rotary, axis=1)
+        for block in range(blocks):
+            out_ref[places_ref[block]] = query[block * rows : (block + 1) * rows].astype(
+                jnp.bfloat16
+            )
+
+    whole = pl.BlockSpec(memory_space=pltpu.VMEM)
+    return pl.pallas_call(
+        body,
+        in_specs=[pl.BlockSpec(memory_space=pltpu.SMEM), whole, whole, whole],
+        out_specs=whole,
+        out_shape=jax.ShapeDtypeStruct((blocks, rows, wide), jnp.bfloat16),
+        cost_estimate=pl.CostEstimate(
+            flops=2 * kept.shape[0] * heads * NOPE * LATENT,
+            bytes_accessed=6 * kept.size + 2 * w_uk.size + 2 * blocks * rows * wide,
+            transcendentals=0,
+        ),
+        compiler_params=pltpu.CompilerParams(vmem_limit_bytes=32 * 1024 * 1024),
+    )(places, kept, away, w_uk)
 
 
 def attend_rows(query, keys, lengths, turn):
@@ -189,20 +227,9 @@
     projected = projected.reshape(nc * nx * nz, nl, local, projected.shape[-1])
     kept = jnp.where(l_index == 0, projected[:, 0], projected[:, 1])
     sent = jnp.where(l_index == 0, projected[:, 1], projected[:, 0]).astype(bf16)
-    projected = kept + shift(sent, "l", 1).astype(jnp.float32)
-    projected = projected.astype(bf16).reshape(-1, heads_here, NOPE + ROPE)
-    absorbed = jnp.einsum(
-        "nhd,hdc->nhc", projected[..., :NOPE], w_uk, preferred_element_type=jnp.float32
-    ).astype(bf16)
-    query = jnp.concatenate(
-        [
-            absorbed.reshape(-1, heads_here * LATENT),
-            projected[..., NOPE:].reshape(-1, heads_here * ROPE),
-        ],
-        axis=1,
-    )
-    query = query.reshape(nc * nx * nz, local, heads_here * (LATENT + ROPE))
-    query = lax.all_to_all(jnp.take(query, turned, axis=0, mode="clip"), HEADS, 0, 0, tiled=True)
+    kept, sent = kept.reshape(-1, kept.shape[-1]), sent.reshape(-1, kept.shape[-1])
+    query = absorb_rows(kept, shift(sent, "l", 1), w_uk, turned.astype(jnp.int32))
+    query = lax.all_to_all(query, HEADS, 0, 0, tiled=True)
 
     fresh = jnp.transpose(fresh_latent, (1, 2, 0))
     keys = jnp.concatenate(
@@ -236,18 +263,16 @@
     head_values = head_values.reshape(nc * nx * nz, local * heads_here * VHEAD)
     head_values = jnp.take(head_values, turned, axis=0, mode="clip").reshape(-1, heads_here * VHEAD)
     terms = jnp.dot(head_values, w_o, preferred_element_type=jnp.float32).astype(bf16)
-    terms, weights = lax.optimization_barrier((terms, weights))
     half = terms.shape[0] // 2
     terms = terms[:half].astype(jnp.float32) + shift(terms[half:], "c", 1).astype(jnp.float32)
-    attention_out = scatter_rows(terms.astype(bf16))
+    terms, weights = lax.optimization_barrier((terms.astype(bf16), weights))
+    attention_out = scatter_rows(terms)
     mixed = (stream.reshape(local, width).astype(jnp.float32) + attention_out).astype(bf16)
     normed = rms_scale(mixed, norm_gain)
 
-    split = normed.reshape(local, ny, nl, chunk)
-    kept = lax.dynamic_index_in_dim(split, l_index, axis=2, keepdims=False)
-    sent = lax.dynamic_index_in_dim(split, 1 - l_index, axis=2, keepdims=False)
-    pair = by_pair(kept.reshape(local, ny * chunk), sent.reshape(local, ny * chunk))
-    first = lax.optimization_barrier(gather_back(jnp.concatenate(pair, axis=0), "z"))
+    split = normed.reshape(local, ny, nl, chunk).transpose(2, 0, 1, 3).reshape(nl, local, -1)
+    sent = jnp.broadcast_to(split[None], (nz,) + split.shape).reshape(nz * nl, local, -1)
+    first = lax.all_to_all(sent, ("z", "l"), 0, 0, tiled=True).reshape(-1, ny * chunk)
     first = lax.optimization_barrier(gather_back(first, "x"))
     second = shift(first, "c", 1)
 
@@ -270,17 +295,13 @@
     first_away, second_away = lax.optimization_barrier((first_away, second_away))
     away = shift(down(second, second_away).astype(bf16), "c", 1)
     terms = down(first, first_away) + away.astype(jnp.float32)
-    value = scatter_rows(terms.astype(bf16))
-    sent = jnp.where(l_index == 0, value[local:], value[:local]).astype(bf16)
-    value = jnp.where(l_index == 0, value[:local], value[local:])
-    sent = shift(sent, "l", 1).astype(jnp.float32)
-    value = jnp.stack(
-        [
-            jnp.where(l_index == 0, value, sent).reshape(local, ny, chunk),
-            jnp.where(l_index == 0, sent, value).reshape(local, ny, chunk),
-        ],
-        axis=2,
-    ).reshape(local, width)
+    rows = terms.shape[0] // nx
+    terms = terms.astype(bf16)
+    terms = scatter_back([terms[k * rows : (k + 1) * rows] for k in range(nx)], "x").astype(bf16)
+    terms = terms.reshape(nz * nl, local, ny * chunk)
+    value = lax.all_to_all(terms, ("z", "l"), 0, 0, tiled=True).astype(jnp.float32)
+    value = jnp.sum(value.reshape(nz, nl, local, ny, chunk), axis=0)
+    value = value.transpose(1, 2, 0, 3).reshape(local, width)
     out = (mixed.astype(jnp.float32) + value).astype(bf16)
     return out.reshape(STEPS, rows_dev, width)
 

time: 225 us -> 220 us (0.978)
  starting transfers between devices: 80.9 us -> 66.9 us
  waiting for transfers between devices: 75.5 us -> 84.8 us
    ppermute x34 -> x26, starting transfers between devices: 68.5 us -> 49.2 us  [shift(): lax.ppermute(value, axis, [(i, (i + by) % size) for i in range(size)])]
    all_to_all x1 -> x2, waiting for transfers between devices: 17 us -> 34.1 us  [the longest x1 17.2 us: shards(): returned = lax.all_to_all(attended, HEADS, 0, 0, tiled=True)]
    ppermute x34 -> x26, waiting for transfers between devices: 56 us -> 48.4 us  [shift(): lax.ppermute(value, axis, [(i, (i + by) % size) for i in range(size)])]
    all_to_all x1 -> x2, starting transfers between devices: 12.4 us -> 17.6 us  [the longest x1 12.4 us: shards(): query = lax.all_to_all(query, HEADS, 0, 0, tiled=True)]
    all_to_all x1 -> x2, blocking collectives: 22.2 us -> 23.4 us  [the longest x1 11.8 us: shards(): lax.all_to_all(terms, ('z', 'l'), 0, 0, tiled=True).astype(jnp.float32)]
  transfers between devices with their start and end apart: 37 -> 30, of which waited for: 24 -> 21; matrix products, arithmetic and copies ran while one was open for 10% -> 9% of each run, Pallas kernels for 1% -> 2%
where the time goes in v1:
time: 220 us; the launch traced here: 219 us
  waiting for transfers between devices  84.8 us (39%)
  starting transfers between devices  66.9 us (30%)
  blocking collectives  23.4 us (11%)
  between operations  14 us (6%)
  matrix products  12.3 us (6%)
  local copies, waits for them, and re-layouts  6.7 us (3%)
  other arithmetic  6.42 us (3%)
  Pallas kernels  4.43 us (2%)
    ppermute x26, starting transfers between devices, shift(): lax.ppermute(value, axis, [(i, (i + by) % size) for i in range(size)])  49.2 us
    ppermute x26, waiting for transfers between devices, shift(): lax.ppermute(value, axis, [(i, (i + by) % size) for i in range(size)])  48.4 us
    all_to_all x1, waiting for transfers between devices, shards(): returned = lax.all_to_all(attended, HEADS, 0, 0, tiled=True)  17.2 us
    all_to_all x1, waiting for transfers between devices, shards(): query = lax.all_to_all(query, HEADS, 0, 0, tiled=True)  16.9 us
    all_to_all x1, starting transfers between devices, shards(): query = lax.all_to_all(query, HEADS, 0, 0, tiled=True)  12.4 us
    all_to_all x1, blocking collectives, shards(): lax.all_to_all(terms, ('z', 'l'), 0, 0, tiled=True).astype(jnp.float32)  11.8 us
    all_to_all x1, blocking collectives, shards(): lax.all_to_all(sent, ('z', 'l'), 0, 0, tiled=True).reshape(-1, ny * chunk)  11.5 us
    all_to_all x1, starting transfers between devices, shards(): returned = lax.all_to_all(attended, HEADS, 0, 0, tiled=True)  5.21 us
  transfers between devices with their start and end apart: 30, of which 21 were waited for; matrix products, arithmetic and copies ran while one was open for 9% of the time, Pallas kernels for 2%

profile of v1, /device:TPU:1, one launch (start us, length us, event | category | flops | bytes accessed | tf_op | source)
XLA Modules:
  0.0 218.9 jit_solution(6609343217925093253)
XLA Ops:
  11.9 3.1 %collective-permute-start.1 = (bf16[8,768]{1,0:T(8,128)(2,1)S(1)}, bf16[8,768]{1,0:T(8,128)(2,1)S(1)}, u32[]{:S(2)}, u32[]{:S(2)}) collective-permute-start(bf16[8,768]{1,0:T(8,128)(2,1)S(1)} %pad_maximum_fusion.3), channel_id=1, source_target_pairs={{0,8},{8,16},{16,24},{24,0},{1,9},{9,17},{17,25},{25,1},{2,10},{10... | collective-permute-start | bytes 36872 | tf_op jit(solution)/shard_map/ppermute | solution.py:24
  14.9 4.9 %collective-permute-start.2 = (bf16[8,768]{1,0:T(8,128)(2,1)S(1)}, bf16[8,768]{1,0:T(8,128)(2,1)S(1)}, u32[]{:S(2)}, u32[]{:S(2)}) collective-permute-start(bf16[8,768]{1,0:T(8,128)(2,1)S(1)} %pad_maximum_fusion.3), channel_id=1, source_target_pairs={{0,16},{8,24},{16,0},{24,8},{1,17},{9,25},{17,1},{25,9},{2,18},{10... | collective-permute-start | bytes 36872 | tf_op jit(solution)/shard_map/ppermute | solution.py:24
  22.2 2.6 %pad_maximum_fusion = bf16[864,896]{1,0:T(8,128)(2,1)} fusion(bf16[288,896]{1,0:T(8,128)(2,1)} %param.25, bf16[288,896]{1,0:T(8,128)(2,1)} %bitcast.83, bf16[288,896]{1,0:T(8,128)(2,1)} %bitcast.84), kind=kLoop, calls=%fused_computation.14 | loop fusion | flops 4644864 | bytes 3096576 | tf_op jit(solution)/shard_map/concatenate | solution.py:221
  32.3 4.1 %collective-permute-start.7 = (bf16[128,768]{1,0:T(8,128)(2,1)S(1)}, bf16[128,768]{1,0:T(8,128)(2,1)S(1)}, u32[]{:S(2)}, u32[]{:S(2)}) collective-permute-start(bf16[128,768]{1,0:T(8,128)(2,1)S(1)} %pad_maximum_fusion.2), channel_id=1, source_target_pairs={{0,1},{1,0},{2,3},{3,2},{4,5},{5,4},{6,7},{7,6},{8,9},{9,8},{10,11... | collective-permute-start | bytes 589832 | tf_op jit(solution)/shard_map/ppermute | solution.py:24
  42.8 3.0 %collective-permute-done.8.away_ref = bf16[128,768]{1,0:T(8,128)(2,1)S(1)} collective-permute-done((bf16[128,768]{1,0:T(8,128)(2,1)S(1)}, bf16[128,768]{1,0:T(8,128)(2,1)S(1)}, u32[]{:S(2)}, u32[]{:S(2)}) %collective-permute-start.8) | collective-permute-done | bytes 196640 | tf_op jit(solution)/shard_map/ppermute | solution.py:24
  47.5 12.4 %all-to-all-start = ((bf16[32,4,2304]{2,1,0:T(4,128)(2,1)}), bf16[32,4,2304]{2,1,0:T(4,128)(2,1)S(1)}, u32[]{:S(2)}, u32[]{:S(2)}) async-start(bf16[32,4,2304]{2,1,0:T(4,128)(2,1)} %shard_map.127), calls=%async_computation | async-start | bytes 1179648 | tf_op jit(solution)/shard_map/all_to_all | solution.py:232
  61.9 16.9 %all-to-all-done = bf16[32,4,2304]{2,1,0:T(4,128)(2,1)S(1)} async-done(((bf16[32,4,2304]{2,1,0:T(4,128)(2,1)}), bf16[32,4,2304]{2,1,0:T(4,128)(2,1)S(1)}, u32[]{:S(2)}, u32[]{:S(2)}) %all-to-all-start) | async-done | bytes 589856 | tf_op jit(solution)/shard_map/all_to_all | solution.py:232
  78.9 2.7 %shard_map.128 = bf16[2,2,32,2048]{3,2,1,0:T(8,128)(2,1)S(1)} custom-call(s32[2]{0:T(128)S(1)} %copy-done.2, bf16[2,2,32,2304]{3,2,1,0:T(8,128)(2,1)S(1)} %bitcast.76, bf16[2,576,640]{2,1,0:T(8,128)(2,1)S(1)} %fusion.10.keys_ref, f32[2,2,2,128]{3,2,1,0:T(2,128)S(1)} %pad_maximum_fusion.4.turn_ref), custom_call_target="tpu_custom_call" | custom-call | flops 536870912 | bytes 2654208 | tf_op jit(solution)/shard_map/pallas_call | solution.py:154
  82.8 5.2 %all-to-all-start.1 = ((bf16[32,4,2048]{2,1,0:T(4,128)(2,1)}), bf16[32,4,2048]{2,1,0:T(4,128)(2,1)S(1)}, u32[]{:S(2)}, u32[]{:S(2)}) async-start(bf16[32,4,2048]{2,1,0:T(4,128)(2,1)} %copy.34), calls=%async_computation.1 | async-start | bytes 1048576 | tf_op jit(solution)/shard_map/all_to_all | solution.py:258
  88.0 17.2 %all-to-all-done.1 = bf16[32,4,2048]{2,1,0:T(4,128)(2,1)S(1)} async-done(((bf16[32,4,2048]{2,1,0:T(4,128)(2,1)}), bf16[32,4,2048]{2,1,0:T(4,128)(2,1)S(1)}, u32[]{:S(2)}, u32[]{:S(2)}) %all-to-all-start.1) | async-done | bytes 524320 | tf_op jit(solution)/shard_map/all_to_all | solution.py:258
  106.8 4.2 %convolution_convert_fusion = bf16[128,7168]{1,0:T(8,128)(2,1)S(1)} fusion(bf16[128,512]{1,0:T(8,128)(2,1)S(1)} %reshape.110, bf16[512,7168]{1,0:T(8,128)(2,1)} %param.21), kind=kOutput, calls=%fused_computation.1 | convolution fusion | flops 940441600 | bytes 9306112 | tf_op jit(solution)/shard_map/dot_general | solution.py:265
  118.6 4.9 %collective-permute-done.10 = bf16[16,7168]{1,0:T(8,128)(2,1)S(1)} collective-permute-done((bf16[16,7168]{1,0:T(8,128)(2,1)S(1)}, bf16[16,7168]{1,0:T(8,128)(2,1)S(1)}, u32[]{:S(2)}, u32[]{:S(2)}) %collective-permute-start.10) | collective-permute-done | bytes 229408 | tf_op jit(solution)/shard_map/ppermute | solution.py:24
  123.5 4.2 %collective-permute-done.12 = bf16[16,7168]{1,0:T(8,128)(2,1)S(1)} collective-permute-done((bf16[16,7168]{1,0:T(8,128)(2,1)S(1)}, bf16[16,7168]{1,0:T(8,128)(2,1)S(1)}, u32[]{:S(2)}, u32[]{:S(2)}) %collective-permute-start.12) | collective-permute-done | bytes 229408 | tf_op jit(solution)/shard_map/ppermute | solution.py:24
  135.7 4.2 %collective-permute-done.15 = bf16[4,7168]{1,0:T(4,128)(2,1)S(1)} collective-permute-done((bf16[4,7168]{1,0:T(4,128)(2,1)S(1)}, bf16[4,7168]{1,0:T(4,128)(2,1)S(1)}, u32[]{:S(2)}, u32[]{:S(2)}) %collective-permute-start.15) | collective-permute-done | bytes 57376 | tf_op jit(solution)/shard_map/ppermute | solution.py:24
  141.3 11.5 %all_to_all.20 = bf16[8,4,3584]{2,1,0:T(4,128)(2,1)S(1)} all-to-all(bf16[8,4,3584]{2,1,0:T(4,128)(2,1)S(1)} %bitcast.82), channel_id=1, replica_groups=mesh['y'=4,'l'=2,'z'=4,'x'=4,'c'=2] {'z','l'}, dimensions={0} | all-to-all | bytes 458752 | tf_op jit(solution)/shard_map/all_to_all | solution.py:275
  153.8 3.0 %collective-permute-start.17 = (bf16[32,3584]{1,0:T(8,128)(2,1)S(1)}, bf16[32,3584]{1,0:T(8,128)(2,1)S(1)}, u32[]{:S(2)}, u32[]{:S(2)}) collective-permute-start(bf16[32,3584]{1,0:T(8,128)(2,1)S(1)} %reshape.113), channel_id=1, source_target_pairs={{0,4},{2,6},{4,0},{6,2},{1,5},{3,7},{5,1},{7,3},{8,12},{10,14},{12... | collective-permute-start | bytes 688136 | tf_op jit(solution)/shard_map/ppermute | solution.py:24
  159.0 3.7 %collective-permute-done.17 = bf16[32,3584]{1,0:T(8,128)(2,1)S(1)} collective-permute-done((bf16[32,3584]{1,0:T(8,128)(2,1)S(1)}, bf16[32,3584]{1,0:T(8,128)(2,1)S(1)}, u32[]{:S(2)}, u32[]{:S(2)}) %collective-permute-start.17) | collective-permute-done | bytes 229408 | tf_op jit(solution)/shard_map/ppermute | solution.py:24
  162.8 5.6 %collective-permute-start.20 = (bf16[128,3584]{1,0:T(8,128)(2,1)S(1)}, bf16[128,3584]{1,0:T(8,128)(2,1)S(1)}, u32[]{:S(2)}, u32[]{:S(2)}) collective-permute-start(bf16[128,3584]{1,0:T(8,128)(2,1)S(1)} %pad_maximum_fusion.1), channel_id=1, source_target_pairs={{0,1},{1,0},{2,3},{3,2},{4,5},{5,4},{6,7},{7,6},{8,9},{9,8},{10,11... | collective-permute-start | bytes 2752520 | tf_op jit(solution)/shard_map/ppermute | solution.py:24
  168.5 3.4 %fusion.30 = (bf16[128,576]{0,1:T(8,128)(2,1)S(1)}, f32[128,576]{0,1:T(8,128)S(1)}) fusion(bf16[128,3584]{1,0:T(8,128)(2,1)S(1)} %pad_maximum_fusion.1, bf16[864,3584]{1,0:T(8,128)(2,1)} %all-gather.5.cloned.1.call-done), kind=kOutput, calls=%fused_computation.69 | convolution fusion | flops 528556032 | bytes 5488640 | tf_op jit(solution)/shard_map/dot_general | solution.py:280
  175.0 2.7 %collective-permute-done.19 = bf16[128,576]{0,1:T(8,128)(2,1)S(1)} collective-permute-done((bf16[128,576]{0,1:T(8,128)(2,1)S(1)}, bf16[128,576]{0,1:T(8,128)(2,1)S(1)}, u32[]{:S(2)}, u32[]{:S(2)}) %collective-permute-start.19) | collective-permute-done | bytes 147488 | tf_op jit(solution)/shard_map/ppermute | solution.py:24
  177.6 3.2 %collective-permute-done.21 = bf16[128,576]{0,1:T(8,128)(2,1)S(1)} collective-permute-done((bf16[128,576]{0,1:T(8,128)(2,1)S(1)}, bf16[128,576]{0,1:T(8,128)(2,1)S(1)}, u32[]{:S(2)}, u32[]{:S(2)}) %collective-permute-start.21) | collective-permute-done | bytes 147488 | tf_op jit(solution)/shard_map/ppermute | solution.py:24
  188.6 4.8 %collective-permute-done.23 = bf16[32,3584]{1,0:T(8,128)(2,1)S(1)} collective-permute-done((bf16[32,3584]{1,0:T(8,128)(2,1)S(1)}, bf16[32,3584]{1,0:T(8,128)(2,1)S(1)}, u32[]{:S(2)}, u32[]{:S(2)}) %collective-permute-start.23) | collective-permute-done | bytes 229408 | tf_op jit(solution)/shard_map/ppermute | solution.py:24
  193.4 5.5 %collective-permute-done.25 = bf16[32,3584]{1,0:T(8,128)(2,1)S(1)} collective-permute-done((bf16[32,3584]{1,0:T(8,128)(2,1)S(1)}, bf16[32,3584]{1,0:T(8,128)(2,1)S(1)}, u32[]{:S(2)}, u32[]{:S(2)}) %collective-permute-start.25) | collective-permute-done | bytes 229408 | tf_op jit(solution)/shard_map/ppermute | solution.py:24
  199.1 11.8 %all_to_all.21 = bf16[8,4,3584]{2,1,0:T(4,128)(2,1)S(1)} all-to-all(bf16[8,4,3584]{2,1,0:T(4,128)(2,1)S(1)} %reshape.114), channel_id=1, replica_groups=mesh['y'=4,'l'=2,'z'=4,'x'=4,'c'=2] {'z','l'}, dimensions={0} | all-to-all | bytes 458752 | tf_op jit(solution)/shard_map/all_to_all | solution.py:302
  (130 shorter events, 59.9 us)
Async XLA Ops:
  6.5 32.5 %all-gather.3.cloned.1.call-start = ((), (), s32[]{:S(2)}) async-start(), calls=%async_computation.4 | async-start | bytes 1474560 | tf_op jit(solution)/shard_map/all_gather | solution.py:214
  7.3 107.7 %all-gather.5.cloned.1.call-start = ((), (), s32[]{:S(2)}) async-start(), calls=%async_computation.5 | async-start | bytes 7741440 | tf_op jit(solution)/shard_map/all_gather | solution.py:223
  11.9 13.0 %collective-permute-start.1 = (bf16[8,768]{1,0:T(8,128)(2,1)S(1)}, bf16[8,768]{1,0:T(8,128)(2,1)S(1)}, u32[]{:S(2)}, u32[]{:S(2)}) collective-permute-start(bf16[8,768]{1,0:T(8,128)(2,1)S(1)} %pad_maximum_fusion.3), channel_id=1, source_target_pairs={{0,8},{8,16},{16,24},{24,0},{1,9},{9,17},{17,25},{25,1},{2,10},{10... | collective-permute-start | bytes 36872 | tf_op jit(solution)/shard_map/ppermute | solution.py:24
  14.9 10.0 %collective-permute-start.2 = (bf16[8,768]{1,0:T(8,128)(2,1)S(1)}, bf16[8,768]{1,0:T(8,128)(2,1)S(1)}, u32[]{:S(2)}, u32[]{:S(2)}) collective-permute-start(bf16[8,768]{1,0:T(8,128)(2,1)S(1)} %pad_maximum_fusion.3), channel_id=1, source_target_pairs={{0,16},{8,24},{16,0},{24,8},{1,17},{9,25},{17,1},{25,9},{2,18},{10... | collective-permute-start | bytes 36872 | tf_op jit(solution)/shard_map/ppermute | solution.py:24
  19.9 5.0 %collective-permute-start.3 = (bf16[8,768]{1,0:T(8,128)(2,1)S(1)}, bf16[8,768]{1,0:T(8,128)(2,1)S(1)}, u32[]{:S(2)}, u32[]{:S(2)}) collective-permute-start(bf16[8,768]{1,0:T(8,128)(2,1)S(1)} %pad_maximum_fusion.3), channel_id=1, source_target_pairs={{0,24},{8,0},{16,8},{24,16},{1,25},{9,1},{17,9},{25,17},{2,26},{10... | collective-permute-start | bytes 36872 | tf_op jit(solution)/shard_map/ppermute | solution.py:24
  25.2 4.9 %collective-permute-start.4 = (bf16[32,768]{1,0:T(8,128)(2,1)S(1)}, bf16[32,768]{1,0:T(8,128)(2,1)S(1)}, u32[]{:S(2)}, u32[]{:S(2)}) collective-permute-start(bf16[32,768]{1,0:T(8,128)(2,1)S(1)} %concatenate.30), channel_id=1, source_target_pairs={{0,2},{2,4},{4,6},{6,0},{1,3},{3,5},{5,7},{7,1},{8,10},{10,12},{12... | collective-permute-start | bytes 147464 | tf_op jit(solution)/shard_map/ppermute | solution.py:24
  32.3 5.2 %collective-permute-start.7 = (bf16[128,768]{1,0:T(8,128)(2,1)S(1)}, bf16[128,768]{1,0:T(8,128)(2,1)S(1)}, u32[]{:S(2)}, u32[]{:S(2)}) collective-permute-start(bf16[128,768]{1,0:T(8,128)(2,1)S(1)} %pad_maximum_fusion.2), channel_id=1, source_target_pairs={{0,1},{1,0},{2,3},{3,2},{4,5},{5,4},{6,7},{7,6},{8,9},{9,8},{10,11... | collective-permute-start | bytes 589832 | tf_op jit(solution)/shard_map/ppermute | solution.py:24
  47.5 31.3 %all-to-all-start = ((bf16[32,4,2304]{2,1,0:T(4,128)(2,1)}), bf16[32,4,2304]{2,1,0:T(4,128)(2,1)S(1)}, u32[]{:S(2)}, u32[]{:S(2)}) async-start(bf16[32,4,2304]{2,1,0:T(4,128)(2,1)} %shard_map.127), calls=%async_computation | async-start | bytes 1179648 | tf_op jit(solution)/shard_map/all_to_all | solution.py:232
  82.8 22.4 %all-to-all-start.1 = ((bf16[32,4,2048]{2,1,0:T(4,128)(2,1)}), bf16[32,4,2048]{2,1,0:T(4,128)(2,1)S(1)}, u32[]{:S(2)}, u32[]{:S(2)}) async-start(bf16[32,4,2048]{2,1,0:T(4,128)(2,1)} %copy.34), calls=%async_computation.1 | async-start | bytes 1048576 | tf_op jit(solution)/shard_map/all_to_all | solution.py:258
  115.1 8.5 %collective-permute-start.10 = (bf16[16,7168]{1,0:T(8,128)(2,1)S(1)}, bf16[16,7168]{1,0:T(8,128)(2,1)S(1)}, u32[]{:S(2)}, u32[]{:S(2)}) collective-permute-start(bf16[16,7168]{1,0:T(8,128)(2,1)S(1)} %get-tuple-element.30), channel_id=1, source_target_pairs={{0,2},{2,4},{4,6},{6,0},{1,3},{3,5},{5,7},{7,1},{8,10},{10,12},{12... | collective-permute-start | bytes 688136 | tf_op jit(solution)/shard_map/ppermute | solution.py:24
  115.9 7.6 %collective-permute-start.11 = (bf16[16,7168]{1,0:T(8,128)(2,1)S(1)}, bf16[16,7168]{1,0:T(8,128)(2,1)S(1)}, u32[]{:S(2)}, u32[]{:S(2)}) collective-permute-start(bf16[16,7168]{1,0:T(8,128)(2,1)S(1)} %get-tuple-element.32), channel_id=1, source_target_pairs={{0,6},{2,0},{4,2},{6,4},{1,7},{3,1},{5,3},{7,5},{8,14},{10,8},{12,... | collective-permute-start | bytes 688136 | tf_op jit(solution)/shard_map/ppermute | solution.py:24
  117.8 9.9 %collective-permute-start.12 = (bf16[16,7168]{1,0:T(8,128)(2,1)S(1)}, bf16[16,7168]{1,0:T(8,128)(2,1)S(1)}, u32[]{:S(2)}, u32[]{:S(2)}) collective-permute-start(bf16[16,7168]{1,0:T(8,128)(2,1)S(1)} %get-tuple-element.31), channel_id=1, source_target_pairs={{0,4},{2,6},{4,0},{6,2},{1,5},{3,7},{5,1},{7,3},{8,12},{10,14},{12... | collective-permute-start | bytes 688136 | tf_op jit(solution)/shard_map/ppermute | solution.py:24
  128.6 5.2 %collective-permute-start.13 = (bf16[4,7168]{1,0:T(4,128)(2,1)S(1)}, bf16[4,7168]{1,0:T(4,128)(2,1)S(1)}, u32[]{:S(2)}, u32[]{:S(2)}) collective-permute-start(bf16[4,7168]{1,0:T(4,128)(2,1)S(1)} %get-tuple-element.33), channel_id=1, source_target_pairs={{0,8},{8,16},{16,24},{24,0},{1,9},{9,17},{17,25},{25,1},{2,10},{10... | collective-permute-start | bytes 172040 | tf_op jit(solution)/shard_map/ppermute | solution.py:24
  130.2 5.5 %collective-permute-start.14 = (bf16[4,7168]{1,0:T(4,128)(2,1)S(1)}, bf16[4,7168]{1,0:T(4,128)(2,1)S(1)}, u32[]{:S(2)}, u32[]{:S(2)}) collective-permute-start(bf16[4,7168]{1,0:T(4,128)(2,1)S(1)} %get-tuple-element.35), channel_id=1, source_target_pairs={{0,24},{8,0},{16,8},{24,16},{1,25},{9,1},{17,9},{25,17},{2,26},{10... | collective-permute-start | bytes 172040 | tf_op jit(solution)/shard_map/ppermute | solution.py:24
  132.3 7.6 %collective-permute-start.15 = (bf16[4,7168]{1,0:T(4,128)(2,1)S(1)}, bf16[4,7168]{1,0:T(4,128)(2,1)S(1)}, u32[]{:S(2)}, u32[]{:S(2)}) collective-permute-start(bf16[4,7168]{1,0:T(4,128)(2,1)S(1)} %get-tuple-element.34), channel_id=1, source_target_pairs={{0,16},{8,24},{16,0},{24,8},{1,17},{9,25},{17,1},{25,9},{2,18},{10... | collective-permute-start | bytes 172040 | tf_op jit(solution)/shard_map/ppermute | solution.py:24
  152.9 6.2 %collective-permute-start.16 = (bf16[32,3584]{1,0:T(8,128)(2,1)S(1)}, bf16[32,3584]{1,0:T(8,128)(2,1)S(1)}, u32[]{:S(2)}, u32[]{:S(2)}) collective-permute-start(bf16[32,3584]{1,0:T(8,128)(2,1)S(1)} %reshape.113), channel_id=1, source_target_pairs={{0,2},{2,4},{4,6},{6,0},{1,3},{3,5},{5,7},{7,1},{8,10},{10,12},{12... | collective-permute-start | bytes 688136 | tf_op jit(solution)/shard_map/ppermute | solution.py:24
  153.8 9.0 %collective-permute-start.17 = (bf16[32,3584]{1,0:T(8,128)(2,1)S(1)}, bf16[32,3584]{1,0:T(8,128)(2,1)S(1)}, u32[]{:S(2)}, u32[]{:S(2)}) collective-permute-start(bf16[32,3584]{1,0:T(8,128)(2,1)S(1)} %reshape.113), channel_id=1, source_target_pairs={{0,4},{2,6},{4,0},{6,2},{1,5},{3,7},{5,1},{7,3},{8,12},{10,14},{12... | collective-permute-start | bytes 688136 | tf_op jit(solution)/shard_map/ppermute | solution.py:24
  156.8 6.0 %collective-permute-start.18 = (bf16[32,3584]{1,0:T(8,128)(2,1)S(1)}, bf16[32,3584]{1,0:T(8,128)(2,1)S(1)}, u32[]{:S(2)}, u32[]{:S(2)}) collective-permute-start(bf16[32,3584]{1,0:T(8,128)(2,1)S(1)} %reshape.113), channel_id=1, source_target_pairs={{0,6},{2,0},{4,2},{6,4},{1,7},{3,1},{5,3},{7,5},{8,14},{10,8},{12,... | collective-permute-start | bytes 688136 | tf_op jit(solution)/shard_map/ppermute | solution.py:24
  162.8 9.4 %collective-permute-start.20 = (bf16[128,3584]{1,0:T(8,128)(2,1)S(1)}, bf16[128,3584]{1,0:T(8,128)(2,1)S(1)}, u32[]{:S(2)}, u32[]{:S(2)}) collective-permute-start(bf16[128,3584]{1,0:T(8,128)(2,1)S(1)} %pad_maximum_fusion.1), channel_id=1, source_target_pairs={{0,1},{1,0},{2,3},{3,2},{4,5},{5,4},{6,7},{7,6},{8,9},{9,8},{10,11... | collective-permute-start | bytes 2752520 | tf_op jit(solution)/shard_map/ppermute | solution.py:24
  171.9 5.8 %collective-permute-start.19 = (bf16[128,576]{0,1:T(8,128)(2,1)S(1)}, bf16[128,576]{0,1:T(8,128)(2,1)S(1)}, u32[]{:S(2)}, u32[]{:S(2)}) collective-permute-start(bf16[128,576]{0,1:T(8,128)(2,1)S(1)} %get-tuple-element.41), channel_id=1, source_target_pairs={{0,32},{32,0},{1,33},{33,1},{2,34},{34,2},{3,35},{35,3},{4,36},{36... | collective-permute-start | bytes 442376 | tf_op jit(solution)/shard_map/ppermute | solution.py:24
  173.5 7.3 %collective-permute-start.21 = (bf16[128,576]{0,1:T(8,128)(2,1)S(1)}, bf16[128,576]{0,1:T(8,128)(2,1)S(1)}, u32[]{:S(2)}, u32[]{:S(2)}) collective-permute-start(bf16[128,576]{0,1:T(8,128)(2,1)S(1)} %get-tuple-element.43), channel_id=1, source_target_pairs={{0,32},{32,0},{1,33},{33,1},{2,34},{34,2},{3,35},{35,3},{4,36},{36... | collective-permute-start | bytes 442376 | tf_op jit(solution)/shard_map/ppermute | solution.py:24
  185.3 8.1 %collective-permute-start.23 = (bf16[32,3584]{1,0:T(8,128)(2,1)S(1)}, bf16[32,3584]{1,0:T(8,128)(2,1)S(1)}, u32[]{:S(2)}, u32[]{:S(2)}) collective-permute-start(bf16[32,3584]{1,0:T(8,128)(2,1)S(1)} %get-tuple-element.27), channel_id=1, source_target_pairs={{0,2},{2,4},{4,6},{6,0},{1,3},{3,5},{5,7},{7,1},{8,10},{10,12},{12... | collective-permute-start | bytes 688136 | tf_op jit(solution)/shard_map/ppermute | solution.py:24
  186.3 7.1 %collective-permute-start.24 = (bf16[32,3584]{1,0:T(8,128)(2,1)S(1)}, bf16[32,3584]{1,0:T(8,128)(2,1)S(1)}, u32[]{:S(2)}, u32[]{:S(2)}) collective-permute-start(bf16[32,3584]{1,0:T(8,128)(2,1)S(1)} %get-tuple-element.29), channel_id=1, source_target_pairs={{0,6},{2,0},{4,2},{6,4},{1,7},{3,1},{5,3},{7,5},{8,14},{10,8},{12,... | collective-permute-start | bytes 688136 | tf_op jit(solution)/shard_map/ppermute | solution.py:24
  188.1 10.8 %collective-permute-start.25 = (bf16[32,3584]{1,0:T(8,128)(2,1)S(1)}, bf16[32,3584]{1,0:T(8,128)(2,1)S(1)}, u32[]{:S(2)}, u32[]{:S(2)}) collective-permute-start(bf16[32,3584]{1,0:T(8,128)(2,1)S(1)} %get-tuple-element.28), channel_id=1, source_target_pairs={{0,4},{2,6},{4,0},{6,2},{1,5},{3,7},{5,1},{7,3},{8,12},{10,14},{12... | collective-permute-start | bytes 688136 | tf_op jit(solution)/shard_map/ppermute | solution.py:24
  (15 other events, 275.8 us)
Sparse Core Ops, SparseCore 0:
  9.2 29.8 all-gather.2
  40.8 68.9 all-gather.4

commit v2 on v1

--- a/solution.py
+++ b/solution.py
@@ -43,14 +43,14 @@
     return total
 
 
-def scatter_rows(terms):
+def scatter_rows(terms, carried):
     for axis in ("x", "z"):
         rows = terms.shape[0] // SIZES[axis]
         parts = [terms[k * rows : (k + 1) * rows] for k in range(SIZES[axis])]
         terms = scatter_back(parts, axis)
         if axis == "x":
-            terms = terms.astype(jnp.bfloat16)
-    return terms
+            terms, carried = lax.optimization_barrier((terms.astype(jnp.bfloat16), carried))
+    return terms, carried
 
 
 def rms_scale(mixed, norm_gain):
@@ -211,7 +211,8 @@
         sent = shift(sent, "l", 1)
         return jnp.where(l_index == 0, kept, sent), jnp.where(l_index == 0, sent, kept)
 
-    query_weights = lax.all_gather(w_qb, "y", axis=0, tiled=True)
+    query_weights = jnp.broadcast_to(w_qb[None], (ny,) + w_qb.shape)
+    query_weights = lax.all_to_all(query_weights, "y", 0, 0, tiled=True).reshape(ny * part, -1)
     split = query_latent.reshape(local, ny, nl, part)
     kept = lax.dynamic_index_in_dim(split, l_index, axis=2, keepdims=False)
     sent = lax.dynamic_index_in_dim(split, 1 - l_index, axis=2, keepdims=False)
@@ -220,8 +221,9 @@
 
     packed = jnp.concatenate([w_gate.T, w_up.T, w_down], axis=0)
     everyone, packed = lax.optimization_barrier((everyone, packed))
-    weights = lax.all_gather(packed, "y", axis=1, tiled=True)
-    everyone = gather_back(gather_back(everyone, "x"), "c")
+    near = (shift(packed, "y", 1), shift(packed, "y", -1))
+    everyone = gather_back(everyone, "x")
+    everyone = gather_back(everyone, "c")
 
     projected = jnp.dot(everyone, query_weights, preferred_element_type=jnp.float32)
     projected = projected.reshape(nc * nx * nz, nl, local, projected.shape[-1])
@@ -256,6 +258,8 @@
     attended = attended.transpose(2, 0, 1, 3).reshape(-1, local, heads_here * LATENT)
 
     returned = lax.all_to_all(attended, HEADS, 0, 0, tiled=True)
+    returned, near = lax.optimization_barrier((returned, near))
+    onward = (near[0][:units], near[1][units : 2 * units], near[0][2 * units :])
     returned = returned.reshape(-1, heads_here, LATENT)
     head_values = jnp.einsum(
         "nhc,hcv->nhv", returned, w_uv, preferred_element_type=jnp.float32
@@ -265,32 +269,49 @@
     terms = jnp.dot(head_values, w_o, preferred_element_type=jnp.float32).astype(bf16)
     half = terms.shape[0] // 2
     terms = terms[:half].astype(jnp.float32) + shift(terms[half:], "c", 1).astype(jnp.float32)
-    terms, weights = lax.optimization_barrier((terms.astype(bf16), weights))
-    attention_out = scatter_rows(terms)
+    attention_out, onward = scatter_rows(terms.astype(bf16), onward)
+    opposite = (shift(onward[0], "y", 1), shift(onward[1], "y", -1))
+    opposite_down = shift(onward[2], "y", 1)
     mixed = (stream.reshape(local, width).astype(jnp.float32) + attention_out).astype(bf16)
     normed = rms_scale(mixed, norm_gain)
 
-    split = normed.reshape(local, ny, nl, chunk).transpose(2, 0, 1, 3).reshape(nl, local, -1)
+    back = jnp.stack([(here["y"] - k) % ny for k in range(ny)])
+    split = jnp.take(normed.reshape(local, ny, nl, chunk), back, axis=1, mode="clip")
+    split = split.transpose(2, 0, 1, 3).reshape(nl, local, -1)
     sent = jnp.broadcast_to(split[None], (nz,) + split.shape).reshape(nz * nl, local, -1)
     first = lax.all_to_all(sent, ("z", "l"), 0, 0, tiled=True).reshape(-1, ny * chunk)
-    first = lax.optimization_barrier(gather_back(first, "x"))
-    second = shift(first, "c", 1)
+    first, opposite = lax.optimization_barrier((first, opposite))
+    first, opposite_down = lax.optimization_barrier((gather_back(first, "x"), opposite_down))
+    opposite = jnp.concatenate(opposite, axis=0)
+    gate_up_parts = (packed[: 2 * units], near[0][: 2 * units], opposite, near[1][: 2 * units])
+    down_parts = (w_down, near[0][2 * units :], opposite_down, near[1][2 * units :])
 
     def gate_up(rows):
-        return lax.dot_general(
-            rows,
-            weights[: 2 * units],
-            (((1,), (1,)), ((), ())),
-            preferred_element_type=jnp.float32,
-        )
+        total = 0.0
+        for k, weights in enumerate(gate_up_parts):
+            total += lax.dot_general(
+                rows[:, k * chunk : (k + 1) * chunk],
+                weights,
+                (((1,), (1,)), ((), ())),
+                preferred_element_type=jnp.float32,
+            )
+        return total
 
     def down(both, away):
         both = both + away.astype(jnp.float32)
         hidden = (jax.nn.silu(both[:, :units]) * both[:, units:]).astype(bf16)
-        return jnp.dot(hidden, weights[2 * units :], preferred_element_type=jnp.float32)
-
-    first, second = gate_up(first), gate_up(second)
+        return jnp.concatenate(
+            [
+                jnp.dot(hidden, weights, preferred_element_type=jnp.float32)
+                for weights in down_parts
+            ],
+            axis=1,
+        )
+
+    second = shift(first, "c", 1)
+    first = gate_up(first)
     first_away = shift(first.astype(bf16), "l", 1)
+    second = gate_up(second)
     second_away = shift(second.astype(bf16), "l", 1)
     first_away, second_away = lax.optimization_barrier((first_away, second_away))
     away = shift(down(second, second_away).astype(bf16), "c", 1)
@@ -301,7 +322,7 @@
     terms = terms.reshape(nz * nl, local, ny * chunk)
     value = lax.all_to_all(terms, ("z", "l"), 0, 0, tiled=True).astype(jnp.float32)
     value = jnp.sum(value.reshape(nz, nl, local, ny, chunk), axis=0)
-    value = value.transpose(1, 2, 0, 3).reshape(local, width)
+    value = jnp.take(value.transpose(1, 2, 0, 3), back, axis=1, mode="clip").reshape(local, width)
     out = (mixed.astype(jnp.float32) + value).astype(bf16)
     return out.reshape(STEPS, rows_dev, width)
 

time: 220 us -> 218 us (level)
  between operations: 14 us -> 0.74 us
  blocking collectives: 23.4 us -> 12.5 us
  matrix products: 12.3 us -> 22.4 us
  local copies, waits for them, and re-layouts: 6.7 us -> 14.4 us
  starting transfers between devices: 66.9 us -> 74.1 us
  waiting for transfers between devices: 84.8 us -> 80.9 us
    all_to_all x1 -> x0, blocking collectives: 11.5 us -> none  [shards(): lax.all_to_all(sent, ('z', 'l'), 0, 0, tiled=True).reshape(-1, ny * chunk)]
    dot_general x4 -> x16, matrix products: 6.03 us -> 17.4 us  [the longest x8 10.8 us: gate_up(): lax.dot_general(rows[:, k * chunk:(k + 1) * chunk], weights, (((1,), (1,)...]
    all_to_all x1, waiting for transfers between devices: 17.2 us -> 7.15 us  [shards(): returned = lax.all_to_all(attended, HEADS, 0, 0, tiled=True)]
    all_to_all x0 -> x2, starting transfers between devices: none -> 8.72 us  [the longest x1 4.54 us: shards(): lax.all_to_all(sent, ('z', 'l'), 0, 0, tiled=True).reshape(-1, ny * chunk)]
    all_to_all x0 -> x2, waiting for transfers between devices: none -> 7.33 us  [the longest x1 7.33 us: shards(): lax.all_to_all(sent, ('z', 'l'), 0, 0, tiled=True).reshape(-1, ny * chunk)]
    ppermute x26 -> x31, waiting for transfers between devices: 48.4 us -> 53.8 us  [shift(): lax.ppermute(value, axis, [(i, (i + by) % size) for i in range(size)])]
    all_to_all x1, waiting for transfers between devices: 16.9 us -> 12.6 us  [shards(): query = lax.all_to_all(query, HEADS, 0, 0, tiled=True)]
    all_to_all x1, starting transfers between devices: 12.4 us -> 8.59 us  [shards(): query = lax.all_to_all(query, HEADS, 0, 0, tiled=True)]
  transfers between devices with their start and end apart: 30 -> 35, of which waited for: 21 -> 20; matrix products, arithmetic and copies ran while one was open for 9% -> 13% of each run, Pallas kernels for 2% -> 1%
where the time goes in v2:
time: 218 us; the launch traced here: 215 us
  waiting for transfers between devices  80.9 us (37%)
  starting transfers between devices  74.1 us (34%)
  matrix products  22.4 us (10%)
  local copies, waits for them, and re-layouts  14.4 us (7%)
  blocking collectives  12.5 us (6%)
  other arithmetic  5.64 us (3%)
  Pallas kernels  4.4 us (2%)
    ppermute x31, waiting for transfers between devices, shift(): lax.ppermute(value, axis, [(i, (i + by) % size) for i in range(size)])  53.8 us
    ppermute x31, starting transfers between devices, shift(): lax.ppermute(value, axis, [(i, (i + by) % size) for i in range(size)])  50.4 us
    all_to_all x1, waiting for transfers between devices, shards(): query = lax.all_to_all(query, HEADS, 0, 0, tiled=True)  12.6 us
    all_to_all x1, blocking collectives, shards(): lax.all_to_all(terms, ('z', 'l'), 0, 0, tiled=True).astype(jnp.float32)  12.5 us
    dot_general x8, matrix products, gate_up(): lax.dot_general(rows[:, k * chunk:(k + 1) * chunk], weights, (((1,), (1,)...  10.8 us
    all_to_all x1, starting transfers between devices, shards(): query = lax.all_to_all(query, HEADS, 0, 0, tiled=True)  8.59 us
    all_to_all x1, waiting for transfers between devices, shards(): lax.all_to_all(sent, ('z', 'l'), 0, 0, tiled=True).reshape(-1, ny * chunk)  7.33 us
    all_to_all x1, waiting for transfers between devices, shards(): returned = lax.all_to_all(attended, HEADS, 0, 0, tiled=True)  7.15 us
  transfers between devices with their start and end apart: 35, of which 20 were waited for; matrix products, arithmetic and copies ran while one was open for 13% of the time, Pallas kernels for 1%

profile of v2, /device:TPU:1, one launch (start us, length us, event | category | flops | bytes accessed | tf_op | source)
XLA Modules:
  0.0 215.2 jit_solution(1370939607433388835)
XLA Ops:
  1.1 2.6 %collective-permute-start = (bf16[4,768]{1,0:T(4,128)(2,1)S(1)}, bf16[4,768]{1,0:T(4,128)(2,1)S(1)}, u32[]{:S(2)}, u32[]{:S(2)}) collective-permute-start(bf16[4,768]{1,0:T(4,128)(2,1)S(1)} %reshape.107), channel_id=1, source_target_pairs={{0,32},{32,0},{1,33},{33,1},{2,34},{34,2},{3,35},{35,3},{4,36},{36... | collective-permute-start | bytes 18440 | tf_op jit(solution)/shard_map/ppermute | solution.py:24
  5.7 4.2 %all-to-all-start = ((bf16[4,192,768]{2,1,0:T(8,128)(2,1)}), bf16[4,192,768]{2,1,0:T(8,128)(2,1)S(1)}, u32[]{:S(2)}, u32[]{:S(2)}) async-start(bf16[4,192,768]{2,1,0:T(8,128)(2,1)} %broadcast_in_dim.15), calls=%async_computation | async-start | bytes 2359296 | tf_op jit(solution)/shard_map/all_to_all | solution.py:215
  10.0 3.1 %collective-permute-start.1 = (bf16[8,768]{1,0:T(8,128)(2,1)S(1)}, bf16[8,768]{1,0:T(8,128)(2,1)S(1)}, u32[]{:S(2)}, u32[]{:S(2)}) collective-permute-start(bf16[8,768]{1,0:T(8,128)(2,1)S(1)} %pad_maximum_fusion.4), channel_id=1, source_target_pairs={{0,8},{8,16},{16,24},{24,0},{1,9},{9,17},{17,25},{25,1},{2,10},{10... | collective-permute-start | bytes 36872 | tf_op jit(solution)/shard_map/ppermute | solution.py:24
  13.1 4.2 %collective-permute-start.2 = (bf16[8,768]{1,0:T(8,128)(2,1)S(1)}, bf16[8,768]{1,0:T(8,128)(2,1)S(1)}, u32[]{:S(2)}, u32[]{:S(2)}) collective-permute-start(bf16[8,768]{1,0:T(8,128)(2,1)S(1)} %pad_maximum_fusion.4), channel_id=1, source_target_pairs={{0,16},{8,24},{16,0},{24,8},{1,17},{9,25},{17,1},{25,9},{2,18},{10... | collective-permute-start | bytes 36872 | tf_op jit(solution)/shard_map/ppermute | solution.py:24
  28.1 4.1 %collective-permute-start.7 = (bf16[128,768]{1,0:T(8,128)(2,1)S(1)}, bf16[128,768]{1,0:T(8,128)(2,1)S(1)}, u32[]{:S(2)}, u32[]{:S(2)}) collective-permute-start(bf16[128,768]{1,0:T(8,128)(2,1)S(1)} %pad_maximum_fusion.3), channel_id=1, source_target_pairs={{0,1},{1,0},{2,3},{3,2},{4,5},{5,4},{6,7},{7,6},{8,9},{9,8},{10,11... | collective-permute-start | bytes 589832 | tf_op jit(solution)/shard_map/ppermute | solution.py:24
  35.4 4.9 %collective-permute-done.8.away_ref = bf16[128,768]{1,0:T(8,128)(2,1)S(1)} collective-permute-done((bf16[128,768]{1,0:T(8,128)(2,1)S(1)}, bf16[128,768]{1,0:T(8,128)(2,1)S(1)}, u32[]{:S(2)}, u32[]{:S(2)}) %collective-permute-start.8) | collective-permute-done | bytes 196640 | tf_op jit(solution)/shard_map/ppermute | solution.py:24
  42.1 8.6 %all-to-all-start.1 = ((bf16[32,4,2304]{2,1,0:T(4,128)(2,1)}), bf16[32,4,2304]{2,1,0:T(4,128)(2,1)S(1)}, u32[]{:S(2)}, u32[]{:S(2)}) async-start(bf16[32,4,2304]{2,1,0:T(4,128)(2,1)} %shard_map.127), calls=%async_computation.1 | async-start | bytes 1179648 | tf_op jit(solution)/shard_map/all_to_all | solution.py:234
  55.7 12.6 %all-to-all-done.1 = bf16[32,4,2304]{2,1,0:T(4,128)(2,1)S(1)} async-done(((bf16[32,4,2304]{2,1,0:T(4,128)(2,1)}), bf16[32,4,2304]{2,1,0:T(4,128)(2,1)S(1)}, u32[]{:S(2)}, u32[]{:S(2)}) %all-to-all-start.1) | async-done | bytes 589856 | tf_op jit(solution)/shard_map/all_to_all | solution.py:234
  68.4 2.7 %shard_map.128 = bf16[2,2,32,2048]{3,2,1,0:T(8,128)(2,1)S(1)} custom-call(s32[2]{0:T(128)S(1)} %copy-done.2, bf16[2,2,32,2304]{3,2,1,0:T(8,128)(2,1)S(1)} %bitcast.90, bf16[2,576,640]{2,1,0:T(8,128)(2,1)S(1)} %fusion.2.keys_ref, f32[2,2,2,128]{3,2,1,0:T(2,128)S(1)} %pad_maximum_fusion.5.turn_ref), custom_call_target="tpu_custom_call" | custom-call | flops 536870912 | bytes 2654208 | tf_op jit(solution)/shard_map/pallas_call | solution.py:154
  72.3 6.4 %all-to-all-start.2 = ((bf16[32,4,2048]{2,1,0:T(4,128)(2,1)}), bf16[32,4,2048]{2,1,0:T(4,128)(2,1)S(1)}, u32[]{:S(2)}, u32[]{:S(2)}) async-start(bf16[32,4,2048]{2,1,0:T(4,128)(2,1)} %copy.47), calls=%async_computation.2 | async-start | bytes 1048576 | tf_op jit(solution)/shard_map/all_to_all | solution.py:260
  78.7 9.4 %collective-permute-done.9 = bf16[864,896]{1,0:T(8,128)(2,1)} collective-permute-done((bf16[864,896]{1,0:T(8,128)(2,1)}, bf16[864,896]{1,0:T(8,128)(2,1)}, u32[]{:S(2)}, u32[]{:S(2)}) %collective-permute-start.9) | collective-permute-done | bytes 1548320 | tf_op jit(solution)/shard_map/ppermute | solution.py:24
  88.2 7.2 %all-to-all-done.2 = bf16[32,4,2048]{2,1,0:T(4,128)(2,1)S(1)} async-done(((bf16[32,4,2048]{2,1,0:T(4,128)(2,1)}), bf16[32,4,2048]{2,1,0:T(4,128)(2,1)S(1)}, u32[]{:S(2)}, u32[]{:S(2)}) %all-to-all-start.2) | async-done | bytes 524320 | tf_op jit(solution)/shard_map/all_to_all | solution.py:260
  96.9 4.2 %convolution_convert_fusion = bf16[128,7168]{1,0:T(8,128)(2,1)S(1)} fusion(bf16[128,512]{1,0:T(8,128)(2,1)S(1)} %reshape.113, bf16[512,7168]{1,0:T(8,128)(2,1)} %param.21), kind=kOutput, calls=%fused_computation.3 | convolution fusion | flops 940441600 | bytes 9306112 | tf_op jit(solution)/shard_map/dot_general | solution.py:269
  106.9 2.5 %collective-permute-start.14 = (bf16[16,7168]{1,0:T(8,128)(2,1)S(1)}, bf16[16,7168]{1,0:T(8,128)(2,1)S(1)}, u32[]{:S(2)}, u32[]{:S(2)}) collective-permute-start(bf16[16,7168]{1,0:T(8,128)(2,1)S(1)} %get-tuple-element.53), channel_id=1, source_target_pairs={{0,4},{2,6},{4,0},{6,2},{1,5},{3,7},{5,1},{7,3},{8,12},{10,14},{12... | collective-permute-start | bytes 688136 | tf_op jit(solution)/shard_map/ppermute | solution.py:24
  112.2 3.0 %collective-permute-done.14 = bf16[16,7168]{1,0:T(8,128)(2,1)S(1)} collective-permute-done((bf16[16,7168]{1,0:T(8,128)(2,1)S(1)}, bf16[16,7168]{1,0:T(8,128)(2,1)S(1)}, u32[]{:S(2)}, u32[]{:S(2)}) %collective-permute-start.14) | collective-permute-done | bytes 229408 | tf_op jit(solution)/shard_map/ppermute | solution.py:24
  115.2 4.3 %collective-permute-done.13 = bf16[16,7168]{1,0:T(8,128)(2,1)S(1)} collective-permute-done((bf16[16,7168]{1,0:T(8,128)(2,1)S(1)}, bf16[16,7168]{1,0:T(8,128)(2,1)S(1)}, u32[]{:S(2)}, u32[]{:S(2)}) %collective-permute-start.13) | collective-permute-done | bytes 229408 | tf_op jit(solution)/shard_map/ppermute | solution.py:24
  123.0 2.8 %collective-permute-start.16 = (bf16[4,7168]{1,0:T(4,128)(2,1)S(1)}, bf16[4,7168]{1,0:T(4,128)(2,1)S(1)}, u32[]{:S(2)}, u32[]{:S(2)}) collective-permute-start(bf16[4,7168]{1,0:T(4,128)(2,1)S(1)} %get-tuple-element.57), channel_id=1, source_target_pairs={{0,24},{8,0},{16,8},{24,16},{1,25},{9,1},{17,9},{25,17},{2,26},{10... | collective-permute-start | bytes 172040 | tf_op jit(solution)/shard_map/ppermute | solution.py:24
  133.0 4.5 %all-to-all-start.3 = ((bf16[8,4,3584]{2,1,0:T(4,128)(2,1)}), bf16[8,4,3584]{2,1,0:T(4,128)(2,1)S(1)}, u32[]{:S(2)}, u32[]{:S(2)}) async-start(bf16[8,4,3584]{2,1,0:T(4,128)(2,1)} %bitcast.52), calls=%async_computation.3 | async-start | bytes 458752 | tf_op jit(solution)/shard_map/all_to_all | solution.py:282
  139.3 7.3 %all-to-all-done.3 = bf16[8,4,3584]{2,1,0:T(4,128)(2,1)S(1)} async-done(((bf16[8,4,3584]{2,1,0:T(4,128)(2,1)}), bf16[8,4,3584]{2,1,0:T(4,128)(2,1)S(1)}, u32[]{:S(2)}, u32[]{:S(2)}) %all-to-all-start.3) | async-done | bytes 229408 | tf_op jit(solution)/shard_map/all_to_all | solution.py:282
  154.2 5.7 %collective-permute-done.20 = bf16[32,3584]{1,0:T(8,128)(2,1)S(1)} collective-permute-done((bf16[32,3584]{1,0:T(8,128)(2,1)S(1)}, bf16[32,3584]{1,0:T(8,128)(2,1)S(1)}, u32[]{:S(2)}, u32[]{:S(2)}) %collective-permute-start.20) | collective-permute-done | bytes 229408 | tf_op jit(solution)/shard_map/ppermute | solution.py:24
  174.8 3.8 %collective-permute-done.26 = bf16[128,576]{0,1:T(8,128)(2,1)S(1)} collective-permute-done((bf16[128,576]{0,1:T(8,128)(2,1)S(1)}, bf16[128,576]{0,1:T(8,128)(2,1)S(1)}, u32[]{:S(2)}, u32[]{:S(2)}) %collective-permute-start.26) | collective-permute-done | bytes 147488 | tf_op jit(solution)/shard_map/ppermute | solution.py:24
  188.9 6.8 %collective-permute-done.30 = bf16[32,3584]{1,0:T(8,128)(2,1)S(1)} collective-permute-done((bf16[32,3584]{1,0:T(8,128)(2,1)S(1)}, bf16[32,3584]{1,0:T(8,128)(2,1)S(1)}, u32[]{:S(2)}, u32[]{:S(2)}) %collective-permute-start.30) | collective-permute-done | bytes 229408 | tf_op jit(solution)/shard_map/ppermute | solution.py:24
  195.8 2.9 %collective-permute-done.29 = bf16[32,3584]{1,0:T(8,128)(2,1)S(1)} collective-permute-done((bf16[32,3584]{1,0:T(8,128)(2,1)S(1)}, bf16[32,3584]{1,0:T(8,128)(2,1)S(1)}, u32[]{:S(2)}, u32[]{:S(2)}) %collective-permute-start.29) | collective-permute-done | bytes 229408 | tf_op jit(solution)/shard_map/ppermute | solution.py:24
  201.1 12.5 %all_to_all.25 = bf16[8,4,3584]{2,1,0:T(4,128)(2,1)S(1)} all-to-all(bf16[8,4,3584]{2,1,0:T(4,128)(2,1)S(1)} %reshape.117), channel_id=1, replica_groups=mesh['y'=4,'l'=2,'z'=4,'x'=4,'c'=2] {'z','l'}, dimensions={0} | all-to-all | bytes 458752 | tf_op jit(solution)/shard_map/all_to_all | solution.py:323
  (162 shorter events, 84.2 us)
Async XLA Ops:
  1.1 8.9 %collective-permute-start = (bf16[4,768]{1,0:T(4,128)(2,1)S(1)}, bf16[4,768]{1,0:T(4,128)(2,1)S(1)}, u32[]{:S(2)}, u32[]{:S(2)}) collective-permute-start(bf16[4,768]{1,0:T(4,128)(2,1)S(1)} %reshape.107), channel_id=1, source_target_pairs={{0,32},{32,0},{1,33},{33,1},{2,34},{34,2},{3,35},{35,3},{4,36},{36... | collective-permute-start | bytes 18440 | tf_op jit(solution)/shard_map/ppermute | solution.py:24
  5.7 27.7 %all-to-all-start = ((bf16[4,192,768]{2,1,0:T(8,128)(2,1)}), bf16[4,192,768]{2,1,0:T(8,128)(2,1)S(1)}, u32[]{:S(2)}, u32[]{:S(2)}) async-start(bf16[4,192,768]{2,1,0:T(8,128)(2,1)} %broadcast_in_dim.15), calls=%async_computation | async-start | bytes 2359296 | tf_op jit(solution)/shard_map/all_to_all | solution.py:215
  10.0 11.1 %collective-permute-start.1 = (bf16[8,768]{1,0:T(8,128)(2,1)S(1)}, bf16[8,768]{1,0:T(8,128)(2,1)S(1)}, u32[]{:S(2)}, u32[]{:S(2)}) collective-permute-start(bf16[8,768]{1,0:T(8,128)(2,1)S(1)} %pad_maximum_fusion.4), channel_id=1, source_target_pairs={{0,8},{8,16},{16,24},{24,0},{1,9},{9,17},{17,25},{25,1},{2,10},{10... | collective-permute-start | bytes 36872 | tf_op jit(solution)/shard_map/ppermute | solution.py:24
  13.1 8.0 %collective-permute-start.2 = (bf16[8,768]{1,0:T(8,128)(2,1)S(1)}, bf16[8,768]{1,0:T(8,128)(2,1)S(1)}, u32[]{:S(2)}, u32[]{:S(2)}) collective-permute-start(bf16[8,768]{1,0:T(8,128)(2,1)S(1)} %pad_maximum_fusion.4), channel_id=1, source_target_pairs={{0,16},{8,24},{16,0},{24,8},{1,17},{9,25},{17,1},{25,9},{2,18},{10... | collective-permute-start | bytes 36872 | tf_op jit(solution)/shard_map/ppermute | solution.py:24
  42.1 26.3 %all-to-all-start.1 = ((bf16[32,4,2304]{2,1,0:T(4,128)(2,1)}), bf16[32,4,2304]{2,1,0:T(4,128)(2,1)S(1)}, u32[]{:S(2)}, u32[]{:S(2)}) async-start(bf16[32,4,2304]{2,1,0:T(4,128)(2,1)} %shard_map.127), calls=%async_computation.1 | async-start | bytes 1179648 | tf_op jit(solution)/shard_map/all_to_all | solution.py:234
  50.7 37.5 %collective-permute-start.9 = (bf16[864,896]{1,0:T(8,128)(2,1)}, bf16[864,896]{1,0:T(8,128)(2,1)}, u32[]{:S(2)}, u32[]{:S(2)}) collective-permute-start(bf16[864,896]{1,0:T(8,128)(2,1)} %pad_maximum_fusion), channel_id=1, source_target_pairs={{0,64},{64,128},{128,192},{192,0},{1,65},{65,129},{129,193},{193,1... | collective-permute-start | bytes 4644872 | tf_op jit(solution)/shard_map/ppermute | solution.py:24
  52.5 35.6 %collective-permute-start.10 = (bf16[864,896]{1,0:T(8,128)(2,1)}, bf16[864,896]{1,0:T(8,128)(2,1)}, u32[]{:S(2)}, u32[]{:S(2)}) collective-permute-start(bf16[864,896]{1,0:T(8,128)(2,1)} %pad_maximum_fusion), channel_id=1, source_target_pairs={{0,192},{64,0},{128,64},{192,128},{1,193},{65,1},{129,65},{193,129... | collective-permute-start | bytes 4644872 | tf_op jit(solution)/shard_map/ppermute | solution.py:24
  72.3 23.0 %all-to-all-start.2 = ((bf16[32,4,2048]{2,1,0:T(4,128)(2,1)}), bf16[32,4,2048]{2,1,0:T(4,128)(2,1)S(1)}, u32[]{:S(2)}, u32[]{:S(2)}) async-start(bf16[32,4,2048]{2,1,0:T(4,128)(2,1)} %copy.47), calls=%async_computation.2 | async-start | bytes 1048576 | tf_op jit(solution)/shard_map/all_to_all | solution.py:260
  106.9 8.3 %collective-permute-start.14 = (bf16[16,7168]{1,0:T(8,128)(2,1)S(1)}, bf16[16,7168]{1,0:T(8,128)(2,1)S(1)}, u32[]{:S(2)}, u32[]{:S(2)}) collective-permute-start(bf16[16,7168]{1,0:T(8,128)(2,1)S(1)} %get-tuple-element.53), channel_id=1, source_target_pairs={{0,4},{2,6},{4,0},{6,2},{1,5},{3,7},{5,1},{7,3},{8,12},{10,14},{12... | collective-permute-start | bytes 688136 | tf_op jit(solution)/shard_map/ppermute | solution.py:24
  109.4 10.0 %collective-permute-start.13 = (bf16[16,7168]{1,0:T(8,128)(2,1)S(1)}, bf16[16,7168]{1,0:T(8,128)(2,1)S(1)}, u32[]{:S(2)}, u32[]{:S(2)}) collective-permute-start(bf16[16,7168]{1,0:T(8,128)(2,1)S(1)} %get-tuple-element.54), channel_id=1, source_target_pairs={{0,6},{2,0},{4,2},{6,4},{1,7},{3,1},{5,3},{7,5},{8,14},{10,8},{12,... | collective-permute-start | bytes 688136 | tf_op jit(solution)/shard_map/ppermute | solution.py:24
  110.5 10.0 %collective-permute-start.12 = (bf16[16,7168]{1,0:T(8,128)(2,1)S(1)}, bf16[16,7168]{1,0:T(8,128)(2,1)S(1)}, u32[]{:S(2)}, u32[]{:S(2)}) collective-permute-start(bf16[16,7168]{1,0:T(8,128)(2,1)S(1)} %get-tuple-element.52), channel_id=1, source_target_pairs={{0,2},{2,4},{4,6},{6,0},{1,3},{3,5},{5,7},{7,1},{8,10},{10,12},{12... | collective-permute-start | bytes 688136 | tf_op jit(solution)/shard_map/ppermute | solution.py:24
  120.7 8.9 %collective-permute-start.17 = (bf16[4,7168]{1,0:T(4,128)(2,1)S(1)}, bf16[4,7168]{1,0:T(4,128)(2,1)S(1)}, u32[]{:S(2)}, u32[]{:S(2)}) collective-permute-start(bf16[4,7168]{1,0:T(4,128)(2,1)S(1)} %get-tuple-element.56), channel_id=1, source_target_pairs={{0,16},{8,24},{16,0},{24,8},{1,17},{9,25},{17,1},{25,9},{2,18},{10... | collective-permute-start | bytes 172040 | tf_op jit(solution)/shard_map/ppermute | solution.py:24
  123.0 8.3 %collective-permute-start.16 = (bf16[4,7168]{1,0:T(4,128)(2,1)S(1)}, bf16[4,7168]{1,0:T(4,128)(2,1)S(1)}, u32[]{:S(2)}, u32[]{:S(2)}) collective-permute-start(bf16[4,7168]{1,0:T(4,128)(2,1)S(1)} %get-tuple-element.57), channel_id=1, source_target_pairs={{0,24},{8,0},{16,8},{24,16},{1,25},{9,1},{17,9},{25,17},{2,26},{10... | collective-permute-start | bytes 172040 | tf_op jit(solution)/shard_map/ppermute | solution.py:24
  125.8 20.9 %collective-permute-start.18 = (bf16[288,896]{1,0:T(8,128)(2,1)S(1)}, bf16[288,896]{1,0:T(8,128)(2,1)S(1)}, u32[]{:S(2)}, u32[]{:S(2)}) collective-permute-start(bf16[288,896]{1,0:T(8,128)(2,1)S(1)} %get-tuple-element.33), channel_id=1, source_target_pairs={{0,64},{64,128},{128,192},{192,0},{1,65},{65,129},{129,193},{193,1... | collective-permute-start | bytes 1548296 | tf_op jit(solution)/shard_map/ppermute | solution.py:24
  127.8 18.9 %collective-permute-start.19 = (bf16[288,896]{1,0:T(8,128)(2,1)}, bf16[288,896]{1,0:T(8,128)(2,1)}, u32[]{:S(2)}, u32[]{:S(2)}) collective-permute-start(bf16[288,896]{1,0:T(8,128)(2,1)} %slice.117), channel_id=1, source_target_pairs={{0,192},{64,0},{128,64},{192,128},{1,193},{65,1},{129,65},{193,129... | collective-permute-start | bytes 1548296 | tf_op jit(solution)/shard_map/ppermute | solution.py:24
  133.0 13.6 %all-to-all-start.3 = ((bf16[8,4,3584]{2,1,0:T(4,128)(2,1)}), bf16[8,4,3584]{2,1,0:T(4,128)(2,1)S(1)}, u32[]{:S(2)}, u32[]{:S(2)}) async-start(bf16[8,4,3584]{2,1,0:T(4,128)(2,1)} %bitcast.52), calls=%async_computation.3 | async-start | bytes 458752 | tf_op jit(solution)/shard_map/all_to_all | solution.py:282
  137.6 22.4 %collective-permute-start.23 = (bf16[288,896]{1,0:T(8,128)(2,1)S(1)}, bf16[288,896]{1,0:T(8,128)(2,1)S(1)}, u32[]{:S(2)}, u32[]{:S(2)}) collective-permute-start(bf16[288,896]{1,0:T(8,128)(2,1)S(1)} %get-tuple-element.36), channel_id=1, source_target_pairs={{0,64},{64,128},{128,192},{192,0},{1,65},{65,129},{129,193},{193,1... | collective-permute-start | bytes 1548296 | tf_op jit(solution)/shard_map/ppermute | solution.py:24
  147.7 6.5 %collective-permute-start.21 = (bf16[32,3584]{1,0:T(8,128)(2,1)S(1)}, bf16[32,3584]{1,0:T(8,128)(2,1)S(1)}, u32[]{:S(2)}, u32[]{:S(2)}) collective-permute-start(bf16[32,3584]{1,0:T(8,128)(2,1)S(1)} %reshape.116), channel_id=1, source_target_pairs={{0,4},{2,6},{4,0},{6,2},{1,5},{3,7},{5,1},{7,3},{8,12},{10,14},{12... | collective-permute-start | bytes 688136 | tf_op jit(solution)/shard_map/ppermute | solution.py:24
  148.1 11.7 %collective-permute-start.20 = (bf16[32,3584]{1,0:T(8,128)(2,1)S(1)}, bf16[32,3584]{1,0:T(8,128)(2,1)S(1)}, u32[]{:S(2)}, u32[]{:S(2)}) collective-permute-start(bf16[32,3584]{1,0:T(8,128)(2,1)S(1)} %reshape.116), channel_id=1, source_target_pairs={{0,2},{2,4},{4,6},{6,0},{1,3},{3,5},{5,7},{7,1},{8,10},{10,12},{12... | collective-permute-start | bytes 688136 | tf_op jit(solution)/shard_map/ppermute | solution.py:24
  159.9 7.9 %collective-permute-start.25 = (bf16[128,3584]{1,0:T(8,128)(2,1)S(1)}, bf16[128,3584]{1,0:T(8,128)(2,1)S(1)}, u32[]{:S(2)}, u32[]{:S(2)}) collective-permute-start(bf16[128,3584]{1,0:T(8,128)(2,1)S(1)} %pad_maximum_fusion.1), channel_id=1, source_target_pairs={{0,1},{1,0},{2,3},{3,2},{4,5},{5,4},{6,7},{7,6},{8,9},{9,8},{10,11... | collective-permute-start | bytes 2752520 | tf_op jit(solution)/shard_map/ppermute | solution.py:24
  167.7 7.1 %collective-permute-start.24 = (bf16[128,576]{0,1:T(8,128)(2,1)S(1)}, bf16[128,576]{0,1:T(8,128)(2,1)S(1)}, u32[]{:S(2)}, u32[]{:S(2)}) collective-permute-start(bf16[128,576]{0,1:T(8,128)(2,1)S(1)} %get-tuple-element.63), channel_id=1, source_target_pairs={{0,32},{32,0},{1,33},{33,1},{2,34},{34,2},{3,35},{35,3},{4,36},{36... | collective-permute-start | bytes 442376 | tf_op jit(solution)/shard_map/ppermute | solution.py:24
  186.9 8.9 %collective-permute-start.30 = (bf16[32,3584]{1,0:T(8,128)(2,1)S(1)}, bf16[32,3584]{1,0:T(8,128)(2,1)S(1)}, u32[]{:S(2)}, u32[]{:S(2)}) collective-permute-start(bf16[32,3584]{1,0:T(8,128)(2,1)S(1)} %get-tuple-element.50), channel_id=1, source_target_pairs={{0,4},{2,6},{4,0},{6,2},{1,5},{3,7},{5,1},{7,3},{8,12},{10,14},{12... | collective-permute-start | bytes 688136 | tf_op jit(solution)/shard_map/ppermute | solution.py:24
  187.4 11.2 %collective-permute-start.29 = (bf16[32,3584]{1,0:T(8,128)(2,1)S(1)}, bf16[32,3584]{1,0:T(8,128)(2,1)S(1)}, u32[]{:S(2)}, u32[]{:S(2)}) collective-permute-start(bf16[32,3584]{1,0:T(8,128)(2,1)S(1)} %get-tuple-element.51), channel_id=1, source_target_pairs={{0,6},{2,0},{4,2},{6,4},{1,7},{3,1},{5,3},{7,5},{8,14},{10,8},{12,... | collective-permute-start | bytes 688136 | tf_op jit(solution)/shard_map/ppermute | solution.py:24
  188.4 12.5 %collective-permute-start.28 = (bf16[32,3584]{1,0:T(8,128)(2,1)S(1)}, bf16[32,3584]{1,0:T(8,128)(2,1)S(1)}, u32[]{:S(2)}, u32[]{:S(2)}) collective-permute-start(bf16[32,3584]{1,0:T(8,128)(2,1)S(1)} %get-tuple-element.49), channel_id=1, source_target_pairs={{0,2},{2,4},{4,6},{6,0},{1,3},{3,5},{5,7},{7,1},{8,10},{10,12},{12... | collective-permute-start | bytes 688136 | tf_op jit(solution)/shard_map/ppermute | solution.py:24
  (21 other events, 256.8 us)

commit v3 on v2

--- a/solution.py
+++ b/solution.py
@@ -259,7 +259,7 @@
 
     returned = lax.all_to_all(attended, HEADS, 0, 0, tiled=True)
     returned, near = lax.optimization_barrier((returned, near))
-    onward = (near[0][:units], near[1][units : 2 * units], near[0][2 * units :])
+    onward = (near[0][:units], near[1][units : 2 * units])
     returned = returned.reshape(-1, heads_here, LATENT)
     head_values = jnp.einsum(
         "nhc,hcv->nhv", returned, w_uv, preferred_element_type=jnp.float32
@@ -271,7 +271,7 @@
     terms = terms[:half].astype(jnp.float32) + shift(terms[half:], "c", 1).astype(jnp.float32)
     attention_out, onward = scatter_rows(terms.astype(bf16), onward)
     opposite = (shift(onward[0], "y", 1), shift(onward[1], "y", -1))
-    opposite_down = shift(onward[2], "y", 1)
+    opposite_down = shift(near[0][2 * units :], "y", 1)
     mixed = (stream.reshape(local, width).astype(jnp.float32) + attention_out).astype(bf16)
     normed = rms_scale(mixed, norm_gain)
 

time: 218 us -> 218 us (level)
  no operation moved by 1% of the time
where the time goes in v3:
time: 218 us; the launch traced here: 215 us
  waiting for transfers between devices  80.9 us (37%)
  starting transfers between devices  74.1 us (34%)
  matrix products  22.4 us (10%)
  local copies, waits for them, and re-layouts  14.4 us (7%)
  blocking collectives  12.5 us (6%)
  other arithmetic  5.64 us (3%)
  Pallas kernels  4.4 us (2%)
    ppermute x31, waiting for transfers between devices, shift(): lax.ppermute(value, axis, [(i, (i + by) % size) for i in range(size)])  53.8 us
    ppermute x31, starting transfers between devices, shift(): lax.ppermute(value, axis, [(i, (i + by) % size) for i in range(size)])  50.4 us
    all_to_all x1, waiting for transfers between devices, shards(): query = lax.all_to_all(query, HEADS, 0, 0, tiled=True)  12.6 us
    all_to_all x1, blocking collectives, shards(): lax.all_to_all(terms, ('z', 'l'), 0, 0, tiled=True).astype(jnp.float32)  12.5 us
    dot_general x8, matrix products, gate_up(): lax.dot_general(rows[:, k * chunk:(k + 1) * chunk], weights, (((1,), (1,)...  10.8 us
    all_to_all x1, starting transfers between devices, shards(): query = lax.all_to_all(query, HEADS, 0, 0, tiled=True)  8.59 us
    all_to_all x1, waiting for transfers between devices, shards(): lax.all_to_all(sent, ('z', 'l'), 0, 0, tiled=True).reshape(-1, ny * chunk)  7.33 us
    all_to_all x1, waiting for transfers between devices, shards(): returned = lax.all_to_all(attended, HEADS, 0, 0, tiled=True)  7.15 us
  transfers between devices with their start and end apart: 35, of which 20 were waited for; matrix products, arithmetic and copies ran while one was open for 13% of the time, Pallas kernels for 1%

profile of v3, /device:TPU:1, one launch (start us, length us, event | category | flops | bytes accessed | tf_op | source)
XLA Modules:
  0.0 215.2 jit_solution(1370939607433388835)
XLA Ops:
  1.1 2.6 %collective-permute-start = (bf16[4,768]{1,0:T(4,128)(2,1)S(1)}, bf16[4,768]{1,0:T(4,128)(2,1)S(1)}, u32[]{:S(2)}, u32[]{:S(2)}) collective-permute-start(bf16[4,768]{1,0:T(4,128)(2,1)S(1)} %reshape.107), channel_id=1, source_target_pairs={{0,32},{32,0},{1,33},{33,1},{2,34},{34,2},{3,35},{35,3},{4,36},{36... | collective-permute-start | bytes 18440 | tf_op jit(solution)/shard_map/ppermute | solution.py:24
  5.7 4.2 %all-to-all-start = ((bf16[4,192,768]{2,1,0:T(8,128)(2,1)}), bf16[4,192,768]{2,1,0:T(8,128)(2,1)S(1)}, u32[]{:S(2)}, u32[]{:S(2)}) async-start(bf16[4,192,768]{2,1,0:T(8,128)(2,1)} %broadcast_in_dim.15), calls=%async_computation | async-start | bytes 2359296 | tf_op jit(solution)/shard_map/all_to_all | solution.py:215
  10.0 3.1 %collective-permute-start.1 = (bf16[8,768]{1,0:T(8,128)(2,1)S(1)}, bf16[8,768]{1,0:T(8,128)(2,1)S(1)}, u32[]{:S(2)}, u32[]{:S(2)}) collective-permute-start(bf16[8,768]{1,0:T(8,128)(2,1)S(1)} %pad_maximum_fusion.4), channel_id=1, source_target_pairs={{0,8},{8,16},{16,24},{24,0},{1,9},{9,17},{17,25},{25,1},{2,10},{10... | collective-permute-start | bytes 36872 | tf_op jit(solution)/shard_map/ppermute | solution.py:24
  13.1 4.2 %collective-permute-start.2 = (bf16[8,768]{1,0:T(8,128)(2,1)S(1)}, bf16[8,768]{1,0:T(8,128)(2,1)S(1)}, u32[]{:S(2)}, u32[]{:S(2)}) collective-permute-start(bf16[8,768]{1,0:T(8,128)(2,1)S(1)} %pad_maximum_fusion.4), channel_id=1, source_target_pairs={{0,16},{8,24},{16,0},{24,8},{1,17},{9,25},{17,1},{25,9},{2,18},{10... | collective-permute-start | bytes 36872 | tf_op jit(solution)/shard_map/ppermute | solution.py:24
  28.1 4.1 %collective-permute-start.7 = (bf16[128,768]{1,0:T(8,128)(2,1)S(1)}, bf16[128,768]{1,0:T(8,128)(2,1)S(1)}, u32[]{:S(2)}, u32[]{:S(2)}) collective-permute-start(bf16[128,768]{1,0:T(8,128)(2,1)S(1)} %pad_maximum_fusion.3), channel_id=1, source_target_pairs={{0,1},{1,0},{2,3},{3,2},{4,5},{5,4},{6,7},{7,6},{8,9},{9,8},{10,11... | collective-permute-start | bytes 589832 | tf_op jit(solution)/shard_map/ppermute | solution.py:24
  35.4 4.9 %collective-permute-done.8.away_ref = bf16[128,768]{1,0:T(8,128)(2,1)S(1)} collective-permute-done((bf16[128,768]{1,0:T(8,128)(2,1)S(1)}, bf16[128,768]{1,0:T(8,128)(2,1)S(1)}, u32[]{:S(2)}, u32[]{:S(2)}) %collective-permute-start.8) | collective-permute-done | bytes 196640 | tf_op jit(solution)/shard_map/ppermute | solution.py:24
  42.1 8.6 %all-to-all-start.1 = ((bf16[32,4,2304]{2,1,0:T(4,128)(2,1)}), bf16[32,4,2304]{2,1,0:T(4,128)(2,1)S(1)}, u32[]{:S(2)}, u32[]{:S(2)}) async-start(bf16[32,4,2304]{2,1,0:T(4,128)(2,1)} %shard_map.127), calls=%async_computation.1 | async-start | bytes 1179648 | tf_op jit(solution)/shard_map/all_to_all | solution.py:234
  55.7 12.6 %all-to-all-done.1 = bf16[32,4,2304]{2,1,0:T(4,128)(2,1)S(1)} async-done(((bf16[32,4,2304]{2,1,0:T(4,128)(2,1)}), bf16[32,4,2304]{2,1,0:T(4,128)(2,1)S(1)}, u32[]{:S(2)}, u32[]{:S(2)}) %all-to-all-start.1) | async-done | bytes 589856 | tf_op jit(solution)/shard_map/all_to_all | solution.py:234
  68.4 2.7 %shard_map.128 = bf16[2,2,32,2048]{3,2,1,0:T(8,128)(2,1)S(1)} custom-call(s32[2]{0:T(128)S(1)} %copy-done.2, bf16[2,2,32,2304]{3,2,1,0:T(8,128)(2,1)S(1)} %bitcast.90, bf16[2,576,640]{2,1,0:T(8,128)(2,1)S(1)} %fusion.2.keys_ref, f32[2,2,2,128]{3,2,1,0:T(2,128)S(1)} %pad_maximum_fusion.5.turn_ref), custom_call_target="tpu_custom_call" | custom-call | flops 536870912 | bytes 2654208 | tf_op jit(solution)/shard_map/pallas_call | solution.py:154
  72.3 6.4 %all-to-all-start.2 = ((bf16[32,4,2048]{2,1,0:T(4,128)(2,1)}), bf16[32,4,2048]{2,1,0:T(4,128)(2,1)S(1)}, u32[]{:S(2)}, u32[]{:S(2)}) async-start(bf16[32,4,2048]{2,1,0:T(4,128)(2,1)} %copy.47), calls=%async_computation.2 | async-start | bytes 1048576 | tf_op jit(solution)/shard_map/all_to_all | solution.py:260
  78.7 9.4 %collective-permute-done.9 = bf16[864,896]{1,0:T(8,128)(2,1)} collective-permute-done((bf16[864,896]{1,0:T(8,128)(2,1)}, bf16[864,896]{1,0:T(8,128)(2,1)}, u32[]{:S(2)}, u32[]{:S(2)}) %collective-permute-start.9) | collective-permute-done | bytes 1548320 | tf_op jit(solution)/shard_map/ppermute | solution.py:24
  88.2 7.2 %all-to-all-done.2 = bf16[32,4,2048]{2,1,0:T(4,128)(2,1)S(1)} async-done(((bf16[32,4,2048]{2,1,0:T(4,128)(2,1)}), bf16[32,4,2048]{2,1,0:T(4,128)(2,1)S(1)}, u32[]{:S(2)}, u32[]{:S(2)}) %all-to-all-start.2) | async-done | bytes 524320 | tf_op jit(solution)/shard_map/all_to_all | solution.py:260
  96.9 4.2 %convolution_convert_fusion = bf16[128,7168]{1,0:T(8,128)(2,1)S(1)} fusion(bf16[128,512]{1,0:T(8,128)(2,1)S(1)} %reshape.113, bf16[512,7168]{1,0:T(8,128)(2,1)} %param.21), kind=kOutput, calls=%fused_computation.3 | convolution fusion | flops 940441600 | bytes 9306112 | tf_op jit(solution)/shard_map/dot_general | solution.py:269
  106.9 2.5 %collective-permute-start.14 = (bf16[16,7168]{1,0:T(8,128)(2,1)S(1)}, bf16[16,7168]{1,0:T(8,128)(2,1)S(1)}, u32[]{:S(2)}, u32[]{:S(2)}) collective-permute-start(bf16[16,7168]{1,0:T(8,128)(2,1)S(1)} %get-tuple-element.51), channel_id=1, source_target_pairs={{0,4},{2,6},{4,0},{6,2},{1,5},{3,7},{5,1},{7,3},{8,12},{10,14},{12... | collective-permute-start | bytes 688136 | tf_op jit(solution)/shard_map/ppermute | solution.py:24
  112.2 3.0 %collective-permute-done.14 = bf16[16,7168]{1,0:T(8,128)(2,1)S(1)} collective-permute-done((bf16[16,7168]{1,0:T(8,128)(2,1)S(1)}, bf16[16,7168]{1,0:T(8,128)(2,1)S(1)}, u32[]{:S(2)}, u32[]{:S(2)}) %collective-permute-start.14) | collective-permute-done | bytes 229408 | tf_op jit(solution)/shard_map/ppermute | solution.py:24
  115.2 4.3 %collective-permute-done.13 = bf16[16,7168]{1,0:T(8,128)(2,1)S(1)} collective-permute-done((bf16[16,7168]{1,0:T(8,128)(2,1)S(1)}, bf16[16,7168]{1,0:T(8,128)(2,1)S(1)}, u32[]{:S(2)}, u32[]{:S(2)}) %collective-permute-start.13) | collective-permute-done | bytes 229408 | tf_op jit(solution)/shard_map/ppermute | solution.py:24
  123.0 2.8 %collective-permute-start.16 = (bf16[4,7168]{1,0:T(4,128)(2,1)S(1)}, bf16[4,7168]{1,0:T(4,128)(2,1)S(1)}, u32[]{:S(2)}, u32[]{:S(2)}) collective-permute-start(bf16[4,7168]{1,0:T(4,128)(2,1)S(1)} %get-tuple-element.55), channel_id=1, source_target_pairs={{0,24},{8,0},{16,8},{24,16},{1,25},{9,1},{17,9},{25,17},{2,26},{10... | collective-permute-start | bytes 172040 | tf_op jit(solution)/shard_map/ppermute | solution.py:24
  133.0 4.5 %all-to-all-start.3 = ((bf16[8,4,3584]{2,1,0:T(4,128)(2,1)}), bf16[8,4,3584]{2,1,0:T(4,128)(2,1)S(1)}, u32[]{:S(2)}, u32[]{:S(2)}) async-start(bf16[8,4,3584]{2,1,0:T(4,128)(2,1)} %bitcast.52), calls=%async_computation.3 | async-start | bytes 458752 | tf_op jit(solution)/shard_map/all_to_all | solution.py:282
  139.3 7.3 %all-to-all-done.3 = bf16[8,4,3584]{2,1,0:T(4,128)(2,1)S(1)} async-done(((bf16[8,4,3584]{2,1,0:T(4,128)(2,1)}), bf16[8,4,3584]{2,1,0:T(4,128)(2,1)S(1)}, u32[]{:S(2)}, u32[]{:S(2)}) %all-to-all-start.3) | async-done | bytes 229408 | tf_op jit(solution)/shard_map/all_to_all | solution.py:282
  154.2 5.7 %collective-permute-done.20 = bf16[32,3584]{1,0:T(8,128)(2,1)S(1)} collective-permute-done((bf16[32,3584]{1,0:T(8,128)(2,1)S(1)}, bf16[32,3584]{1,0:T(8,128)(2,1)S(1)}, u32[]{:S(2)}, u32[]{:S(2)}) %collective-permute-start.20) | collective-permute-done | bytes 229408 | tf_op jit(solution)/shard_map/ppermute | solution.py:24
  174.8 3.8 %collective-permute-done.26 = bf16[128,576]{0,1:T(8,128)(2,1)S(1)} collective-permute-done((bf16[128,576]{0,1:T(8,128)(2,1)S(1)}, bf16[128,576]{0,1:T(8,128)(2,1)S(1)}, u32[]{:S(2)}, u32[]{:S(2)}) %collective-permute-start.26) | collective-permute-done | bytes 147488 | tf_op jit(solution)/shard_map/ppermute | solution.py:24
  188.9 6.8 %collective-permute-done.30 = bf16[32,3584]{1,0:T(8,128)(2,1)S(1)} collective-permute-done((bf16[32,3584]{1,0:T(8,128)(2,1)S(1)}, bf16[32,3584]{1,0:T(8,128)(2,1)S(1)}, u32[]{:S(2)}, u32[]{:S(2)}) %collective-permute-start.30) | collective-permute-done | bytes 229408 | tf_op jit(solution)/shard_map/ppermute | solution.py:24
  195.8 2.9 %collective-permute-done.29 = bf16[32,3584]{1,0:T(8,128)(2,1)S(1)} collective-permute-done((bf16[32,3584]{1,0:T(8,128)(2,1)S(1)}, bf16[32,3584]{1,0:T(8,128)(2,1)S(1)}, u32[]{:S(2)}, u32[]{:S(2)}) %collective-permute-start.29) | collective-permute-done | bytes 229408 | tf_op jit(solution)/shard_map/ppermute | solution.py:24
  201.1 12.5 %all_to_all.25 = bf16[8,4,3584]{2,1,0:T(4,128)(2,1)S(1)} all-to-all(bf16[8,4,3584]{2,1,0:T(4,128)(2,1)S(1)} %reshape.117), channel_id=1, replica_groups=mesh['y'=4,'l'=2,'z'=4,'x'=4,'c'=2] {'z','l'}, dimensions={0} | all-to-all | bytes 458752 | tf_op jit(solution)/shard_map/all_to_all | solution.py:323
  (162 shorter events, 84.2 us)
Async XLA Ops:
  1.1 8.9 %collective-permute-start = (bf16[4,768]{1,0:T(4,128)(2,1)S(1)}, bf16[4,768]{1,0:T(4,128)(2,1)S(1)}, u32[]{:S(2)}, u32[]{:S(2)}) collective-permute-start(bf16[4,768]{1,0:T(4,128)(2,1)S(1)} %reshape.107), channel_id=1, source_target_pairs={{0,32},{32,0},{1,33},{33,1},{2,34},{34,2},{3,35},{35,3},{4,36},{36... | collective-permute-start | bytes 18440 | tf_op jit(solution)/shard_map/ppermute | solution.py:24
  5.7 27.7 %all-to-all-start = ((bf16[4,192,768]{2,1,0:T(8,128)(2,1)}), bf16[4,192,768]{2,1,0:T(8,128)(2,1)S(1)}, u32[]{:S(2)}, u32[]{:S(2)}) async-start(bf16[4,192,768]{2,1,0:T(8,128)(2,1)} %broadcast_in_dim.15), calls=%async_computation | async-start | bytes 2359296 | tf_op jit(solution)/shard_map/all_to_all | solution.py:215
  10.0 11.1 %collective-permute-start.1 = (bf16[8,768]{1,0:T(8,128)(2,1)S(1)}, bf16[8,768]{1,0:T(8,128)(2,1)S(1)}, u32[]{:S(2)}, u32[]{:S(2)}) collective-permute-start(bf16[8,768]{1,0:T(8,128)(2,1)S(1)} %pad_maximum_fusion.4), channel_id=1, source_target_pairs={{0,8},{8,16},{16,24},{24,0},{1,9},{9,17},{17,25},{25,1},{2,10},{10... | collective-permute-start | bytes 36872 | tf_op jit(solution)/shard_map/ppermute | solution.py:24
  13.1 8.0 %collective-permute-start.2 = (bf16[8,768]{1,0:T(8,128)(2,1)S(1)}, bf16[8,768]{1,0:T(8,128)(2,1)S(1)}, u32[]{:S(2)}, u32[]{:S(2)}) collective-permute-start(bf16[8,768]{1,0:T(8,128)(2,1)S(1)} %pad_maximum_fusion.4), channel_id=1, source_target_pairs={{0,16},{8,24},{16,0},{24,8},{1,17},{9,25},{17,1},{25,9},{2,18},{10... | collective-permute-start | bytes 36872 | tf_op jit(solution)/shard_map/ppermute | solution.py:24
  42.1 26.3 %all-to-all-start.1 = ((bf16[32,4,2304]{2,1,0:T(4,128)(2,1)}), bf16[32,4,2304]{2,1,0:T(4,128)(2,1)S(1)}, u32[]{:S(2)}, u32[]{:S(2)}) async-start(bf16[32,4,2304]{2,1,0:T(4,128)(2,1)} %shard_map.127), calls=%async_computation.1 | async-start | bytes 1179648 | tf_op jit(solution)/shard_map/all_to_all | solution.py:234
  50.7 37.5 %collective-permute-start.9 = (bf16[864,896]{1,0:T(8,128)(2,1)}, bf16[864,896]{1,0:T(8,128)(2,1)}, u32[]{:S(2)}, u32[]{:S(2)}) collective-permute-start(bf16[864,896]{1,0:T(8,128)(2,1)} %pad_maximum_fusion), channel_id=1, source_target_pairs={{0,64},{64,128},{128,192},{192,0},{1,65},{65,129},{129,193},{193,1... | collective-permute-start | bytes 4644872 | tf_op jit(solution)/shard_map/ppermute | solution.py:24
  52.5 35.6 %collective-permute-start.10 = (bf16[864,896]{1,0:T(8,128)(2,1)}, bf16[864,896]{1,0:T(8,128)(2,1)}, u32[]{:S(2)}, u32[]{:S(2)}) collective-permute-start(bf16[864,896]{1,0:T(8,128)(2,1)} %pad_maximum_fusion), channel_id=1, source_target_pairs={{0,192},{64,0},{128,64},{192,128},{1,193},{65,1},{129,65},{193,129... | collective-permute-start | bytes 4644872 | tf_op jit(solution)/shard_map/ppermute | solution.py:24
  72.3 23.0 %all-to-all-start.2 = ((bf16[32,4,2048]{2,1,0:T(4,128)(2,1)}), bf16[32,4,2048]{2,1,0:T(4,128)(2,1)S(1)}, u32[]{:S(2)}, u32[]{:S(2)}) async-start(bf16[32,4,2048]{2,1,0:T(4,128)(2,1)} %copy.47), calls=%async_computation.2 | async-start | bytes 1048576 | tf_op jit(solution)/shard_map/all_to_all | solution.py:260
  106.9 8.3 %collective-permute-start.14 = (bf16[16,7168]{1,0:T(8,128)(2,1)S(1)}, bf16[16,7168]{1,0:T(8,128)(2,1)S(1)}, u32[]{:S(2)}, u32[]{:S(2)}) collective-permute-start(bf16[16,7168]{1,0:T(8,128)(2,1)S(1)} %get-tuple-element.51), channel_id=1, source_target_pairs={{0,4},{2,6},{4,0},{6,2},{1,5},{3,7},{5,1},{7,3},{8,12},{10,14},{12... | collective-permute-start | bytes 688136 | tf_op jit(solution)/shard_map/ppermute | solution.py:24
  109.4 10.0 %collective-permute-start.13 = (bf16[16,7168]{1,0:T(8,128)(2,1)S(1)}, bf16[16,7168]{1,0:T(8,128)(2,1)S(1)}, u32[]{:S(2)}, u32[]{:S(2)}) collective-permute-start(bf16[16,7168]{1,0:T(8,128)(2,1)S(1)} %get-tuple-element.52), channel_id=1, source_target_pairs={{0,6},{2,0},{4,2},{6,4},{1,7},{3,1},{5,3},{7,5},{8,14},{10,8},{12,... | collective-permute-start | bytes 688136 | tf_op jit(solution)/shard_map/ppermute | solution.py:24
  110.5 10.0 %collective-permute-start.12 = (bf16[16,7168]{1,0:T(8,128)(2,1)S(1)}, bf16[16,7168]{1,0:T(8,128)(2,1)S(1)}, u32[]{:S(2)}, u32[]{:S(2)}) collective-permute-start(bf16[16,7168]{1,0:T(8,128)(2,1)S(1)} %get-tuple-element.50), channel_id=1, source_target_pairs={{0,2},{2,4},{4,6},{6,0},{1,3},{3,5},{5,7},{7,1},{8,10},{10,12},{12... | collective-permute-start | bytes 688136 | tf_op jit(solution)/shard_map/ppermute | solution.py:24
  120.7 8.9 %collective-permute-start.17 = (bf16[4,7168]{1,0:T(4,128)(2,1)S(1)}, bf16[4,7168]{1,0:T(4,128)(2,1)S(1)}, u32[]{:S(2)}, u32[]{:S(2)}) collective-permute-start(bf16[4,7168]{1,0:T(4,128)(2,1)S(1)} %get-tuple-element.54), channel_id=1, source_target_pairs={{0,16},{8,24},{16,0},{24,8},{1,17},{9,25},{17,1},{25,9},{2,18},{10... | collective-permute-start | bytes 172040 | tf_op jit(solution)/shard_map/ppermute | solution.py:24
  123.0 8.3 %collective-permute-start.16 = (bf16[4,7168]{1,0:T(4,128)(2,1)S(1)}, bf16[4,7168]{1,0:T(4,128)(2,1)S(1)}, u32[]{:S(2)}, u32[]{:S(2)}) collective-permute-start(bf16[4,7168]{1,0:T(4,128)(2,1)S(1)} %get-tuple-element.55), channel_id=1, source_target_pairs={{0,24},{8,0},{16,8},{24,16},{1,25},{9,1},{17,9},{25,17},{2,26},{10... | collective-permute-start | bytes 172040 | tf_op jit(solution)/shard_map/ppermute | solution.py:24
  125.8 20.9 %collective-permute-start.18 = (bf16[288,896]{1,0:T(8,128)(2,1)S(1)}, bf16[288,896]{1,0:T(8,128)(2,1)S(1)}, u32[]{:S(2)}, u32[]{:S(2)}) collective-permute-start(bf16[288,896]{1,0:T(8,128)(2,1)S(1)} %get-tuple-element.32), channel_id=1, source_target_pairs={{0,64},{64,128},{128,192},{192,0},{1,65},{65,129},{129,193},{193,1... | collective-permute-start | bytes 1548296 | tf_op jit(solution)/shard_map/ppermute | solution.py:24
  127.8 18.9 %collective-permute-start.19 = (bf16[288,896]{1,0:T(8,128)(2,1)}, bf16[288,896]{1,0:T(8,128)(2,1)}, u32[]{:S(2)}, u32[]{:S(2)}) collective-permute-start(bf16[288,896]{1,0:T(8,128)(2,1)} %slice.117), channel_id=1, source_target_pairs={{0,192},{64,0},{128,64},{192,128},{1,193},{65,1},{129,65},{193,129... | collective-permute-start | bytes 1548296 | tf_op jit(solution)/shard_map/ppermute | solution.py:24
  133.0 13.6 %all-to-all-start.3 = ((bf16[8,4,3584]{2,1,0:T(4,128)(2,1)}), bf16[8,4,3584]{2,1,0:T(4,128)(2,1)S(1)}, u32[]{:S(2)}, u32[]{:S(2)}) async-start(bf16[8,4,3584]{2,1,0:T(4,128)(2,1)} %bitcast.52), calls=%async_computation.3 | async-start | bytes 458752 | tf_op jit(solution)/shard_map/all_to_all | solution.py:282
  137.6 22.4 %collective-permute-start.23 = (bf16[288,896]{1,0:T(8,128)(2,1)S(1)}, bf16[288,896]{1,0:T(8,128)(2,1)S(1)}, u32[]{:S(2)}, u32[]{:S(2)}) collective-permute-start(bf16[288,896]{1,0:T(8,128)(2,1)S(1)} %get-tuple-element.45), channel_id=1, source_target_pairs={{0,64},{64,128},{128,192},{192,0},{1,65},{65,129},{129,193},{193,1... | collective-permute-start | bytes 1548296 | tf_op jit(solution)/shard_map/ppermute | solution.py:24
  147.7 6.5 %collective-permute-start.21 = (bf16[32,3584]{1,0:T(8,128)(2,1)S(1)}, bf16[32,3584]{1,0:T(8,128)(2,1)S(1)}, u32[]{:S(2)}, u32[]{:S(2)}) collective-permute-start(bf16[32,3584]{1,0:T(8,128)(2,1)S(1)} %reshape.116), channel_id=1, source_target_pairs={{0,4},{2,6},{4,0},{6,2},{1,5},{3,7},{5,1},{7,3},{8,12},{10,14},{12... | collective-permute-start | bytes 688136 | tf_op jit(solution)/shard_map/ppermute | solution.py:24
  148.1 11.7 %collective-permute-start.20 = (bf16[32,3584]{1,0:T(8,128)(2,1)S(1)}, bf16[32,3584]{1,0:T(8,128)(2,1)S(1)}, u32[]{:S(2)}, u32[]{:S(2)}) collective-permute-start(bf16[32,3584]{1,0:T(8,128)(2,1)S(1)} %reshape.116), channel_id=1, source_target_pairs={{0,2},{2,4},{4,6},{6,0},{1,3},{3,5},{5,7},{7,1},{8,10},{10,12},{12... | collective-permute-start | bytes 688136 | tf_op jit(solution)/shard_map/ppermute | solution.py:24
  159.9 7.9 %collective-permute-start.25 = (bf16[128,3584]{1,0:T(8,128)(2,1)S(1)}, bf16[128,3584]{1,0:T(8,128)(2,1)S(1)}, u32[]{:S(2)}, u32[]{:S(2)}) collective-permute-start(bf16[128,3584]{1,0:T(8,128)(2,1)S(1)} %pad_maximum_fusion.1), channel_id=1, source_target_pairs={{0,1},{1,0},{2,3},{3,2},{4,5},{5,4},{6,7},{7,6},{8,9},{9,8},{10,11... | collective-permute-start | bytes 2752520 | tf_op jit(solution)/shard_map/ppermute | solution.py:24
  167.7 7.1 %collective-permute-start.24 = (bf16[128,576]{0,1:T(8,128)(2,1)S(1)}, bf16[128,576]{0,1:T(8,128)(2,1)S(1)}, u32[]{:S(2)}, u32[]{:S(2)}) collective-permute-start(bf16[128,576]{0,1:T(8,128)(2,1)S(1)} %get-tuple-element.61), channel_id=1, source_target_pairs={{0,32},{32,0},{1,33},{33,1},{2,34},{34,2},{3,35},{35,3},{4,36},{36... | collective-permute-start | bytes 442376 | tf_op jit(solution)/shard_map/ppermute | solution.py:24
  186.9 8.9 %collective-permute-start.30 = (bf16[32,3584]{1,0:T(8,128)(2,1)S(1)}, bf16[32,3584]{1,0:T(8,128)(2,1)S(1)}, u32[]{:S(2)}, u32[]{:S(2)}) collective-permute-start(bf16[32,3584]{1,0:T(8,128)(2,1)S(1)} %get-tuple-element.48), channel_id=1, source_target_pairs={{0,4},{2,6},{4,0},{6,2},{1,5},{3,7},{5,1},{7,3},{8,12},{10,14},{12... | collective-permute-start | bytes 688136 | tf_op jit(solution)/shard_map/ppermute | solution.py:24
  187.4 11.2 %collective-permute-start.29 = (bf16[32,3584]{1,0:T(8,128)(2,1)S(1)}, bf16[32,3584]{1,0:T(8,128)(2,1)S(1)}, u32[]{:S(2)}, u32[]{:S(2)}) collective-permute-start(bf16[32,3584]{1,0:T(8,128)(2,1)S(1)} %get-tuple-element.49), channel_id=1, source_target_pairs={{0,6},{2,0},{4,2},{6,4},{1,7},{3,1},{5,3},{7,5},{8,14},{10,8},{12,... | collective-permute-start | bytes 688136 | tf_op jit(solution)/shard_map/ppermute | solution.py:24
  188.4 12.5 %collective-permute-start.28 = (bf16[32,3584]{1,0:T(8,128)(2,1)S(1)}, bf16[32,3584]{1,0:T(8,128)(2,1)S(1)}, u32[]{:S(2)}, u32[]{:S(2)}) collective-permute-start(bf16[32,3584]{1,0:T(8,128)(2,1)S(1)} %get-tuple-element.47), channel_id=1, source_target_pairs={{0,2},{2,4},{4,6},{6,0},{1,3},{3,5},{5,7},{7,1},{8,10},{10,12},{12... | collective-permute-start | bytes 688136 | tf_op jit(solution)/shard_map/ppermute | solution.py:24
  (21 other events, 256.8 us)

commit v4 on v3

--- a/solution.py
+++ b/solution.py
@@ -211,13 +211,14 @@
         sent = shift(sent, "l", 1)
         return jnp.where(l_index == 0, kept, sent), jnp.where(l_index == 0, sent, kept)
 
-    query_weights = jnp.broadcast_to(w_qb[None], (ny,) + w_qb.shape)
-    query_weights = lax.all_to_all(query_weights, "y", 0, 0, tiled=True).reshape(ny * part, -1)
     split = query_latent.reshape(local, ny, nl, part)
     kept = lax.dynamic_index_in_dim(split, l_index, axis=2, keepdims=False)
     sent = lax.dynamic_index_in_dim(split, 1 - l_index, axis=2, keepdims=False)
     pair = by_pair(kept.reshape(local, ny * part), sent.reshape(local, ny * part))
-    everyone = gather_back(jnp.concatenate(pair, axis=0), "z")
+    pair, w_qb = lax.optimization_barrier((jnp.concatenate(pair, axis=0), w_qb))
+    everyone = gather_back(pair, "z")
+    query_weights = jnp.broadcast_to(w_qb[None], (ny,) + w_qb.shape)
+    query_weights = lax.all_to_all(query_weights, "y", 0, 0, tiled=True).reshape(ny * part, -1)
 
     packed = jnp.concatenate([w_gate.T, w_up.T, w_down], axis=0)
     everyone, packed = lax.optimization_barrier((everyone, packed))

time: 218 us -> 218 us (level)
  waiting for transfers between devices: 80.9 us -> 83.2 us
    ppermute x31, starting transfers between devices: 50.4 us -> 47.7 us  [shift(): lax.ppermute(value, axis, [(i, (i + by) % size) for i in range(size)])]
    all_to_all x1, starting transfers between devices: 8.59 us -> 11.1 us  [shards(): query = lax.all_to_all(query, HEADS, 0, 0, tiled=True)]
  transfers between devices with their start and end apart: 35 -> 35, of which waited for: 20 -> 21; matrix products, arithmetic and copies ran while one was open for 13% -> 13% of each run, Pallas kernels for 1% -> 1%
where the time goes in v4:
time: 218 us; the launch traced here: 217 us
  waiting for transfers between devices  83.2 us (38%)
  starting transfers between devices  73.5 us (34%)
  matrix products  22.4 us (10%)
  local copies, waits for them, and re-layouts  14.4 us (7%)
  blocking collectives  12.5 us (6%)
  other arithmetic  5.65 us (3%)
  Pallas kernels  4.39 us (2%)
    ppermute x31, waiting for transfers between devices, shift(): lax.ppermute(value, axis, [(i, (i + by) % size) for i in range(size)])  53.5 us
    ppermute x31, starting transfers between devices, shift(): lax.ppermute(value, axis, [(i, (i + by) % size) for i in range(size)])  47.7 us
    all_to_all x1, waiting for transfers between devices, shards(): query = lax.all_to_all(query, HEADS, 0, 0, tiled=True)  13.3 us
    all_to_all x1, blocking collectives, shards(): lax.all_to_all(terms, ('z', 'l'), 0, 0, tiled=True).astype(jnp.float32)  12.5 us
    all_to_all x1, starting transfers between devices, shards(): query = lax.all_to_all(query, HEADS, 0, 0, tiled=True)  11.1 us
    dot_general x8, matrix products, gate_up(): lax.dot_general(rows[:, k * chunk:(k + 1) * chunk], weights, (((1,), (1,)...  10.8 us
    all_to_all x1, waiting for transfers between devices, shards(): lax.all_to_all(sent, ('z', 'l'), 0, 0, tiled=True).reshape(-1, ny * chunk)  8.81 us
    all_to_all x1, waiting for transfers between devices, shards(): returned = lax.all_to_all(attended, HEADS, 0, 0, tiled=True)  7.6 us
  transfers between devices with their start and end apart: 35, of which 21 were waited for; matrix products, arithmetic and copies ran while one was open for 13% of the time, Pallas kernels for 1%

profile of v4, /device:TPU:1, one launch (start us, length us, event | category | flops | bytes accessed | tf_op | source)
XLA Modules:
  0.0 216.9 jit_solution(11764966042089616855)
XLA Ops:
  1.1 2.5 %collective-permute-start = (bf16[4,768]{1,0:T(4,128)(2,1)S(1)}, bf16[4,768]{1,0:T(4,128)(2,1)S(1)}, u32[]{:S(2)}, u32[]{:S(2)}) collective-permute-start(bf16[4,768]{1,0:T(4,128)(2,1)S(1)} %reshape.107), channel_id=1, source_target_pairs={{0,32},{32,0},{1,33},{33,1},{2,34},{34,2},{3,35},{35,3},{4,36},{36... | collective-permute-start | bytes 18440 | tf_op jit(solution)/shard_map/ppermute | solution.py:24
  4.6 5.9 %collective-permute-start.3 = (bf16[8,768]{1,0:T(8,128)(2,1)S(1)}, bf16[8,768]{1,0:T(8,128)(2,1)S(1)}, u32[]{:S(2)}, u32[]{:S(2)}) collective-permute-start(bf16[8,768]{1,0:T(8,128)(2,1)S(1)} %pad_maximum_fusion.5), channel_id=1, source_target_pairs={{0,24},{8,0},{16,8},{24,16},{1,25},{9,1},{17,9},{25,17},{2,26},{10... | collective-permute-start | bytes 36872 | tf_op jit(solution)/shard_map/ppermute | solution.py:24
  15.9 4.2 %all-to-all-start = ((bf16[4,192,768]{2,1,0:T(8,128)(2,1)}), bf16[4,192,768]{2,1,0:T(8,128)(2,1)S(1)}, u32[]{:S(2)}, u32[]{:S(2)}) async-start(bf16[4,192,768]{2,1,0:T(8,128)(2,1)} %broadcast_in_dim.15), calls=%async_computation | async-start | bytes 2359296 | tf_op jit(solution)/shard_map/all_to_all | solution.py:221
  28.5 4.4 %collective-permute-start.7 = (bf16[128,768]{1,0:T(8,128)(2,1)S(1)}, bf16[128,768]{1,0:T(8,128)(2,1)S(1)}, u32[]{:S(2)}, u32[]{:S(2)}) collective-permute-start(bf16[128,768]{1,0:T(8,128)(2,1)S(1)} %pad_maximum_fusion.3), channel_id=1, source_target_pairs={{0,1},{1,0},{2,3},{3,2},{4,5},{5,4},{6,7},{7,6},{8,9},{9,8},{10,11... | collective-permute-start | bytes 589832 | tf_op jit(solution)/shard_map/ppermute | solution.py:24
  36.2 3.3 %collective-permute-done.8.away_ref = bf16[128,768]{1,0:T(8,128)(2,1)S(1)} collective-permute-done((bf16[128,768]{1,0:T(8,128)(2,1)S(1)}, bf16[128,768]{1,0:T(8,128)(2,1)S(1)}, u32[]{:S(2)}, u32[]{:S(2)}) %collective-permute-start.8) | collective-permute-done | bytes 196640 | tf_op jit(solution)/shard_map/ppermute | solution.py:24
  41.3 11.1 %all-to-all-start.1 = ((bf16[32,4,2304]{2,1,0:T(4,128)(2,1)}), bf16[32,4,2304]{2,1,0:T(4,128)(2,1)S(1)}, u32[]{:S(2)}, u32[]{:S(2)}) async-start(bf16[32,4,2304]{2,1,0:T(4,128)(2,1)} %shard_map.127), calls=%async_computation.1 | async-start | bytes 1179648 | tf_op jit(solution)/shard_map/all_to_all | solution.py:235
  57.0 13.3 %all-to-all-done.1 = bf16[32,4,2304]{2,1,0:T(4,128)(2,1)S(1)} async-done(((bf16[32,4,2304]{2,1,0:T(4,128)(2,1)}), bf16[32,4,2304]{2,1,0:T(4,128)(2,1)S(1)}, u32[]{:S(2)}, u32[]{:S(2)}) %all-to-all-start.1) | async-done | bytes 589856 | tf_op jit(solution)/shard_map/all_to_all | solution.py:235
  70.4 2.7 %shard_map.128 = bf16[2,2,32,2048]{3,2,1,0:T(8,128)(2,1)S(1)} custom-call(s32[2]{0:T(128)S(1)} %copy-done.2, bf16[2,2,32,2304]{3,2,1,0:T(8,128)(2,1)S(1)} %bitcast.90, bf16[2,576,640]{2,1,0:T(8,128)(2,1)S(1)} %fusion.2.keys_ref, f32[2,2,2,128]{3,2,1,0:T(2,128)S(1)} %pad_maximum_fusion.6.turn_ref), custom_call_target="tpu_custom_call" | custom-call | flops 536870912 | bytes 2654208 | tf_op jit(solution)/shard_map/pallas_call | solution.py:154
  74.3 6.1 %all-to-all-start.2 = ((bf16[32,4,2048]{2,1,0:T(4,128)(2,1)}), bf16[32,4,2048]{2,1,0:T(4,128)(2,1)S(1)}, u32[]{:S(2)}, u32[]{:S(2)}) async-start(bf16[32,4,2048]{2,1,0:T(4,128)(2,1)} %copy.47), calls=%async_computation.2 | async-start | bytes 1048576 | tf_op jit(solution)/shard_map/all_to_all | solution.py:261
  80.4 8.8 %collective-permute-done.9 = bf16[864,896]{1,0:T(8,128)(2,1)} collective-permute-done((bf16[864,896]{1,0:T(8,128)(2,1)}, bf16[864,896]{1,0:T(8,128)(2,1)}, u32[]{:S(2)}, u32[]{:S(2)}) %collective-permute-start.9) | collective-permute-done | bytes 1548320 | tf_op jit(solution)/shard_map/ppermute | solution.py:24
  89.2 7.6 %all-to-all-done.2 = bf16[32,4,2048]{2,1,0:T(4,128)(2,1)S(1)} async-done(((bf16[32,4,2048]{2,1,0:T(4,128)(2,1)}), bf16[32,4,2048]{2,1,0:T(4,128)(2,1)S(1)}, u32[]{:S(2)}, u32[]{:S(2)}) %all-to-all-start.2) | async-done | bytes 524320 | tf_op jit(solution)/shard_map/all_to_all | solution.py:261
  98.4 4.2 %convolution_convert_fusion = bf16[128,7168]{1,0:T(8,128)(2,1)S(1)} fusion(bf16[128,512]{1,0:T(8,128)(2,1)S(1)} %reshape.113, bf16[512,7168]{1,0:T(8,128)(2,1)} %param.21), kind=kOutput, calls=%fused_computation.3 | convolution fusion | flops 940441600 | bytes 9306112 | tf_op jit(solution)/shard_map/dot_general | solution.py:270
  108.6 2.6 %collective-permute-start.14 = (bf16[16,7168]{1,0:T(8,128)(2,1)S(1)}, bf16[16,7168]{1,0:T(8,128)(2,1)S(1)}, u32[]{:S(2)}, u32[]{:S(2)}) collective-permute-start(bf16[16,7168]{1,0:T(8,128)(2,1)S(1)} %get-tuple-element.55), channel_id=1, source_target_pairs={{0,4},{2,6},{4,0},{6,2},{1,5},{3,7},{5,1},{7,3},{8,12},{10,14},{12... | collective-permute-start | bytes 688136 | tf_op jit(solution)/shard_map/ppermute | solution.py:24
  113.9 3.0 %collective-permute-done.14 = bf16[16,7168]{1,0:T(8,128)(2,1)S(1)} collective-permute-done((bf16[16,7168]{1,0:T(8,128)(2,1)S(1)}, bf16[16,7168]{1,0:T(8,128)(2,1)S(1)}, u32[]{:S(2)}, u32[]{:S(2)}) %collective-permute-start.14) | collective-permute-done | bytes 229408 | tf_op jit(solution)/shard_map/ppermute | solution.py:24
  116.9 4.3 %collective-permute-done.13 = bf16[16,7168]{1,0:T(8,128)(2,1)S(1)} collective-permute-done((bf16[16,7168]{1,0:T(8,128)(2,1)S(1)}, bf16[16,7168]{1,0:T(8,128)(2,1)S(1)}, u32[]{:S(2)}, u32[]{:S(2)}) %collective-permute-start.13) | collective-permute-done | bytes 229408 | tf_op jit(solution)/shard_map/ppermute | solution.py:24
  124.7 2.7 %collective-permute-start.16 = (bf16[4,7168]{1,0:T(4,128)(2,1)S(1)}, bf16[4,7168]{1,0:T(4,128)(2,1)S(1)}, u32[]{:S(2)}, u32[]{:S(2)}) collective-permute-start(bf16[4,7168]{1,0:T(4,128)(2,1)S(1)} %get-tuple-element.59), channel_id=1, source_target_pairs={{0,24},{8,0},{16,8},{24,16},{1,25},{9,1},{17,9},{25,17},{2,26},{10... | collective-permute-start | bytes 172040 | tf_op jit(solution)/shard_map/ppermute | solution.py:24
  130.1 2.9 %collective-permute-done.16 = bf16[4,7168]{1,0:T(4,128)(2,1)S(1)} collective-permute-done((bf16[4,7168]{1,0:T(4,128)(2,1)S(1)}, bf16[4,7168]{1,0:T(4,128)(2,1)S(1)}, u32[]{:S(2)}, u32[]{:S(2)}) %collective-permute-start.16) | collective-permute-done | bytes 57376 | tf_op jit(solution)/shard_map/ppermute | solution.py:24
  134.8 4.5 %all-to-all-start.3 = ((bf16[8,4,3584]{2,1,0:T(4,128)(2,1)}), bf16[8,4,3584]{2,1,0:T(4,128)(2,1)S(1)}, u32[]{:S(2)}, u32[]{:S(2)}) async-start(bf16[8,4,3584]{2,1,0:T(4,128)(2,1)} %bitcast.52), calls=%async_computation.3 | async-start | bytes 458752 | tf_op jit(solution)/shard_map/all_to_all | solution.py:283
  139.5 8.8 %all-to-all-done.3 = bf16[8,4,3584]{2,1,0:T(4,128)(2,1)S(1)} async-done(((bf16[8,4,3584]{2,1,0:T(4,128)(2,1)}), bf16[8,4,3584]{2,1,0:T(4,128)(2,1)S(1)}, u32[]{:S(2)}, u32[]{:S(2)}) %all-to-all-start.3) | async-done | bytes 229408 | tf_op jit(solution)/shard_map/all_to_all | solution.py:283
  155.8 5.8 %collective-permute-done.20 = bf16[32,3584]{1,0:T(8,128)(2,1)S(1)} collective-permute-done((bf16[32,3584]{1,0:T(8,128)(2,1)S(1)}, bf16[32,3584]{1,0:T(8,128)(2,1)S(1)}, u32[]{:S(2)}, u32[]{:S(2)}) %collective-permute-start.20) | collective-permute-done | bytes 229408 | tf_op jit(solution)/shard_map/ppermute | solution.py:24
  176.4 3.8 %collective-permute-done.26 = bf16[128,576]{0,1:T(8,128)(2,1)S(1)} collective-permute-done((bf16[128,576]{0,1:T(8,128)(2,1)S(1)}, bf16[128,576]{0,1:T(8,128)(2,1)S(1)}, u32[]{:S(2)}, u32[]{:S(2)}) %collective-permute-start.26) | collective-permute-done | bytes 147488 | tf_op jit(solution)/shard_map/ppermute | solution.py:24
  190.6 6.8 %collective-permute-done.30 = bf16[32,3584]{1,0:T(8,128)(2,1)S(1)} collective-permute-done((bf16[32,3584]{1,0:T(8,128)(2,1)S(1)}, bf16[32,3584]{1,0:T(8,128)(2,1)S(1)}, u32[]{:S(2)}, u32[]{:S(2)}) %collective-permute-start.30) | collective-permute-done | bytes 229408 | tf_op jit(solution)/shard_map/ppermute | solution.py:24
  197.4 2.9 %collective-permute-done.29 = bf16[32,3584]{1,0:T(8,128)(2,1)S(1)} collective-permute-done((bf16[32,3584]{1,0:T(8,128)(2,1)S(1)}, bf16[32,3584]{1,0:T(8,128)(2,1)S(1)}, u32[]{:S(2)}, u32[]{:S(2)}) %collective-permute-start.29) | collective-permute-done | bytes 229408 | tf_op jit(solution)/shard_map/ppermute | solution.py:24
  202.8 12.5 %all_to_all.25 = bf16[8,4,3584]{2,1,0:T(4,128)(2,1)S(1)} all-to-all(bf16[8,4,3584]{2,1,0:T(4,128)(2,1)S(1)} %reshape.117), channel_id=1, replica_groups=mesh['y'=4,'l'=2,'z'=4,'x'=4,'c'=2] {'z','l'}, dimensions={0} | all-to-all | bytes 458752 | tf_op jit(solution)/shard_map/all_to_all | solution.py:324
  (162 shorter events, 81.6 us)
Async XLA Ops:
  4.6 16.8 %collective-permute-start.3 = (bf16[8,768]{1,0:T(8,128)(2,1)S(1)}, bf16[8,768]{1,0:T(8,128)(2,1)S(1)}, u32[]{:S(2)}, u32[]{:S(2)}) collective-permute-start(bf16[8,768]{1,0:T(8,128)(2,1)S(1)} %pad_maximum_fusion.5), channel_id=1, source_target_pairs={{0,24},{8,0},{16,8},{24,16},{1,25},{9,1},{17,9},{25,17},{2,26},{10... | collective-permute-start | bytes 36872 | tf_op jit(solution)/shard_map/ppermute | solution.py:24
  10.6 10.9 %collective-permute-start.2 = (bf16[8,768]{1,0:T(8,128)(2,1)S(1)}, bf16[8,768]{1,0:T(8,128)(2,1)S(1)}, u32[]{:S(2)}, u32[]{:S(2)}) collective-permute-start(bf16[8,768]{1,0:T(8,128)(2,1)S(1)} %pad_maximum_fusion.5), channel_id=1, source_target_pairs={{0,16},{8,24},{16,0},{24,8},{1,17},{9,25},{17,1},{25,9},{2,18},{10... | collective-permute-start | bytes 36872 | tf_op jit(solution)/shard_map/ppermute | solution.py:24
  11.6 9.9 %collective-permute-start.1 = (bf16[8,768]{1,0:T(8,128)(2,1)S(1)}, bf16[8,768]{1,0:T(8,128)(2,1)S(1)}, u32[]{:S(2)}, u32[]{:S(2)}) collective-permute-start(bf16[8,768]{1,0:T(8,128)(2,1)S(1)} %pad_maximum_fusion.5), channel_id=1, source_target_pairs={{0,8},{8,16},{16,24},{24,0},{1,9},{9,17},{17,25},{25,1},{2,10},{10... | collective-permute-start | bytes 36872 | tf_op jit(solution)/shard_map/ppermute | solution.py:24
  15.9 18.3 %all-to-all-start = ((bf16[4,192,768]{2,1,0:T(8,128)(2,1)}), bf16[4,192,768]{2,1,0:T(8,128)(2,1)S(1)}, u32[]{:S(2)}, u32[]{:S(2)}) async-start(bf16[4,192,768]{2,1,0:T(8,128)(2,1)} %broadcast_in_dim.15), calls=%async_computation | async-start | bytes 2359296 | tf_op jit(solution)/shard_map/all_to_all | solution.py:221
  41.3 29.1 %all-to-all-start.1 = ((bf16[32,4,2304]{2,1,0:T(4,128)(2,1)}), bf16[32,4,2304]{2,1,0:T(4,128)(2,1)S(1)}, u32[]{:S(2)}, u32[]{:S(2)}) async-start(bf16[32,4,2304]{2,1,0:T(4,128)(2,1)} %shard_map.127), calls=%async_computation.1 | async-start | bytes 1179648 | tf_op jit(solution)/shard_map/all_to_all | solution.py:235
  52.4 36.8 %collective-permute-start.9 = (bf16[864,896]{1,0:T(8,128)(2,1)}, bf16[864,896]{1,0:T(8,128)(2,1)}, u32[]{:S(2)}, u32[]{:S(2)}) collective-permute-start(bf16[864,896]{1,0:T(8,128)(2,1)} %pad_maximum_fusion), channel_id=1, source_target_pairs={{0,64},{64,128},{128,192},{192,0},{1,65},{65,129},{129,193},{193,1... | collective-permute-start | bytes 4644872 | tf_op jit(solution)/shard_map/ppermute | solution.py:24
  52.7 36.5 %collective-permute-start.10 = (bf16[864,896]{1,0:T(8,128)(2,1)}, bf16[864,896]{1,0:T(8,128)(2,1)}, u32[]{:S(2)}, u32[]{:S(2)}) collective-permute-start(bf16[864,896]{1,0:T(8,128)(2,1)} %pad_maximum_fusion), channel_id=1, source_target_pairs={{0,192},{64,0},{128,64},{192,128},{1,193},{65,1},{129,65},{193,129... | collective-permute-start | bytes 4644872 | tf_op jit(solution)/shard_map/ppermute | solution.py:24
  74.3 22.5 %all-to-all-start.2 = ((bf16[32,4,2048]{2,1,0:T(4,128)(2,1)}), bf16[32,4,2048]{2,1,0:T(4,128)(2,1)S(1)}, u32[]{:S(2)}, u32[]{:S(2)}) async-start(bf16[32,4,2048]{2,1,0:T(4,128)(2,1)} %copy.47), calls=%async_computation.2 | async-start | bytes 1048576 | tf_op jit(solution)/shard_map/all_to_all | solution.py:261
  108.6 8.3 %collective-permute-start.14 = (bf16[16,7168]{1,0:T(8,128)(2,1)S(1)}, bf16[16,7168]{1,0:T(8,128)(2,1)S(1)}, u32[]{:S(2)}, u32[]{:S(2)}) collective-permute-start(bf16[16,7168]{1,0:T(8,128)(2,1)S(1)} %get-tuple-element.55), channel_id=1, source_target_pairs={{0,4},{2,6},{4,0},{6,2},{1,5},{3,7},{5,1},{7,3},{8,12},{10,14},{12... | collective-permute-start | bytes 688136 | tf_op jit(solution)/shard_map/ppermute | solution.py:24
  111.1 10.0 %collective-permute-start.13 = (bf16[16,7168]{1,0:T(8,128)(2,1)S(1)}, bf16[16,7168]{1,0:T(8,128)(2,1)S(1)}, u32[]{:S(2)}, u32[]{:S(2)}) collective-permute-start(bf16[16,7168]{1,0:T(8,128)(2,1)S(1)} %get-tuple-element.56), channel_id=1, source_target_pairs={{0,6},{2,0},{4,2},{6,4},{1,7},{3,1},{5,3},{7,5},{8,14},{10,8},{12,... | collective-permute-start | bytes 688136 | tf_op jit(solution)/shard_map/ppermute | solution.py:24
  112.3 10.0 %collective-permute-start.12 = (bf16[16,7168]{1,0:T(8,128)(2,1)S(1)}, bf16[16,7168]{1,0:T(8,128)(2,1)S(1)}, u32[]{:S(2)}, u32[]{:S(2)}) collective-permute-start(bf16[16,7168]{1,0:T(8,128)(2,1)S(1)} %get-tuple-element.54), channel_id=1, source_target_pairs={{0,2},{2,4},{4,6},{6,0},{1,3},{3,5},{5,7},{7,1},{8,10},{10,12},{12... | collective-permute-start | bytes 688136 | tf_op jit(solution)/shard_map/ppermute | solution.py:24
  122.4 7.7 %collective-permute-start.17 = (bf16[4,7168]{1,0:T(4,128)(2,1)S(1)}, bf16[4,7168]{1,0:T(4,128)(2,1)S(1)}, u32[]{:S(2)}, u32[]{:S(2)}) collective-permute-start(bf16[4,7168]{1,0:T(4,128)(2,1)S(1)} %get-tuple-element.58), channel_id=1, source_target_pairs={{0,16},{8,24},{16,0},{24,8},{1,17},{9,25},{17,1},{25,9},{2,18},{10... | collective-permute-start | bytes 172040 | tf_op jit(solution)/shard_map/ppermute | solution.py:24
  124.7 8.4 %collective-permute-start.16 = (bf16[4,7168]{1,0:T(4,128)(2,1)S(1)}, bf16[4,7168]{1,0:T(4,128)(2,1)S(1)}, u32[]{:S(2)}, u32[]{:S(2)}) collective-permute-start(bf16[4,7168]{1,0:T(4,128)(2,1)S(1)} %get-tuple-element.59), channel_id=1, source_target_pairs={{0,24},{8,0},{16,8},{24,16},{1,25},{9,1},{17,9},{25,17},{2,26},{10... | collective-permute-start | bytes 172040 | tf_op jit(solution)/shard_map/ppermute | solution.py:24
  127.4 21.0 %collective-permute-start.18 = (bf16[288,896]{1,0:T(8,128)(2,1)S(1)}, bf16[288,896]{1,0:T(8,128)(2,1)S(1)}, u32[]{:S(2)}, u32[]{:S(2)}) collective-permute-start(bf16[288,896]{1,0:T(8,128)(2,1)S(1)} %get-tuple-element.36), channel_id=1, source_target_pairs={{0,64},{64,128},{128,192},{192,0},{1,65},{65,129},{129,193},{193,1... | collective-permute-start | bytes 1548296 | tf_op jit(solution)/shard_map/ppermute | solution.py:24
  127.9 20.5 %collective-permute-start.19 = (bf16[288,896]{1,0:T(8,128)(2,1)}, bf16[288,896]{1,0:T(8,128)(2,1)}, u32[]{:S(2)}, u32[]{:S(2)}) collective-permute-start(bf16[288,896]{1,0:T(8,128)(2,1)} %slice.117), channel_id=1, source_target_pairs={{0,192},{64,0},{128,64},{192,128},{1,193},{65,1},{129,65},{193,129... | collective-permute-start | bytes 1548296 | tf_op jit(solution)/shard_map/ppermute | solution.py:24
  134.8 13.5 %all-to-all-start.3 = ((bf16[8,4,3584]{2,1,0:T(4,128)(2,1)}), bf16[8,4,3584]{2,1,0:T(4,128)(2,1)S(1)}, u32[]{:S(2)}, u32[]{:S(2)}) async-start(bf16[8,4,3584]{2,1,0:T(4,128)(2,1)} %bitcast.52), calls=%async_computation.3 | async-start | bytes 458752 | tf_op jit(solution)/shard_map/all_to_all | solution.py:283
  139.3 22.4 %collective-permute-start.23 = (bf16[288,896]{1,0:T(8,128)(2,1)S(1)}, bf16[288,896]{1,0:T(8,128)(2,1)S(1)}, u32[]{:S(2)}, u32[]{:S(2)}) collective-permute-start(bf16[288,896]{1,0:T(8,128)(2,1)S(1)} %get-tuple-element.49), channel_id=1, source_target_pairs={{0,64},{64,128},{128,192},{192,0},{1,65},{65,129},{129,193},{193,1... | collective-permute-start | bytes 1548296 | tf_op jit(solution)/shard_map/ppermute | solution.py:24
  149.4 6.5 %collective-permute-start.21 = (bf16[32,3584]{1,0:T(8,128)(2,1)S(1)}, bf16[32,3584]{1,0:T(8,128)(2,1)S(1)}, u32[]{:S(2)}, u32[]{:S(2)}) collective-permute-start(bf16[32,3584]{1,0:T(8,128)(2,1)S(1)} %reshape.116), channel_id=1, source_target_pairs={{0,4},{2,6},{4,0},{6,2},{1,5},{3,7},{5,1},{7,3},{8,12},{10,14},{12... | collective-permute-start | bytes 688136 | tf_op jit(solution)/shard_map/ppermute | solution.py:24
  149.7 11.9 %collective-permute-start.20 = (bf16[32,3584]{1,0:T(8,128)(2,1)S(1)}, bf16[32,3584]{1,0:T(8,128)(2,1)S(1)}, u32[]{:S(2)}, u32[]{:S(2)}) collective-permute-start(bf16[32,3584]{1,0:T(8,128)(2,1)S(1)} %reshape.116), channel_id=1, source_target_pairs={{0,2},{2,4},{4,6},{6,0},{1,3},{3,5},{5,7},{7,1},{8,10},{10,12},{12... | collective-permute-start | bytes 688136 | tf_op jit(solution)/shard_map/ppermute | solution.py:24
  161.7 7.8 %collective-permute-start.25 = (bf16[128,3584]{1,0:T(8,128)(2,1)S(1)}, bf16[128,3584]{1,0:T(8,128)(2,1)S(1)}, u32[]{:S(2)}, u32[]{:S(2)}) collective-permute-start(bf16[128,3584]{1,0:T(8,128)(2,1)S(1)} %pad_maximum_fusion.1), channel_id=1, source_target_pairs={{0,1},{1,0},{2,3},{3,2},{4,5},{5,4},{6,7},{7,6},{8,9},{9,8},{10,11... | collective-permute-start | bytes 2752520 | tf_op jit(solution)/shard_map/ppermute | solution.py:24
  169.4 7.1 %collective-permute-start.24 = (bf16[128,576]{0,1:T(8,128)(2,1)S(1)}, bf16[128,576]{0,1:T(8,128)(2,1)S(1)}, u32[]{:S(2)}, u32[]{:S(2)}) collective-permute-start(bf16[128,576]{0,1:T(8,128)(2,1)S(1)} %get-tuple-element.65), channel_id=1, source_target_pairs={{0,32},{32,0},{1,33},{33,1},{2,34},{34,2},{3,35},{35,3},{4,36},{36... | collective-permute-start | bytes 442376 | tf_op jit(solution)/shard_map/ppermute | solution.py:24
  188.6 8.9 %collective-permute-start.30 = (bf16[32,3584]{1,0:T(8,128)(2,1)S(1)}, bf16[32,3584]{1,0:T(8,128)(2,1)S(1)}, u32[]{:S(2)}, u32[]{:S(2)}) collective-permute-start(bf16[32,3584]{1,0:T(8,128)(2,1)S(1)} %get-tuple-element.52), channel_id=1, source_target_pairs={{0,4},{2,6},{4,0},{6,2},{1,5},{3,7},{5,1},{7,3},{8,12},{10,14},{12... | collective-permute-start | bytes 688136 | tf_op jit(solution)/shard_map/ppermute | solution.py:24
  189.2 11.2 %collective-permute-start.29 = (bf16[32,3584]{1,0:T(8,128)(2,1)S(1)}, bf16[32,3584]{1,0:T(8,128)(2,1)S(1)}, u32[]{:S(2)}, u32[]{:S(2)}) collective-permute-start(bf16[32,3584]{1,0:T(8,128)(2,1)S(1)} %get-tuple-element.53), channel_id=1, source_target_pairs={{0,6},{2,0},{4,2},{6,4},{1,7},{3,1},{5,3},{7,5},{8,14},{10,8},{12,... | collective-permute-start | bytes 688136 | tf_op jit(solution)/shard_map/ppermute | solution.py:24
  190.1 12.5 %collective-permute-start.28 = (bf16[32,3584]{1,0:T(8,128)(2,1)S(1)}, bf16[32,3584]{1,0:T(8,128)(2,1)S(1)}, u32[]{:S(2)}, u32[]{:S(2)}) collective-permute-start(bf16[32,3584]{1,0:T(8,128)(2,1)S(1)} %get-tuple-element.51), channel_id=1, source_target_pairs={{0,2},{2,4},{4,6},{6,0},{1,3},{3,5},{5,7},{7,1},{8,10},{10,12},{12... | collective-permute-start | bytes 688136 | tf_op jit(solution)/shard_map/ppermute | solution.py:24
  (21 other events, 247.8 us)
